TPU v7x, 32 devices: a whole 2x2x4 slice. The times are simulated.
32 devices in a mesh: gx: 16 (over z, x, core), gy: 2 (over y).
Axes of the slice: x: 2, y: 2, z: 4, core: 2. Of those that a mesh axis runs over, the one named last changes fastest.
Arguments:
- state: float32 [512, 128, 384], P('gx', 'gy'), may hold values from -3 to 3
- obs_owner: int32 [2, 4096], replicated, may hold values from 0 to 31
- obs_cell: int32 [2, 4096], replicated, may hold values from 0 to 2047
- obs_level: int32 [2, 4096], replicated, may hold values from 0 to 3
- obs_coef: float32 [2, 3, 4096], replicated, may hold values from -1 to 1
- obs_value: float32 [2, 4096], replicated, may hold values from -8 to 8
- obs_error: float32 [2, 4096], replicated, may hold values from 0.5 to 2
- pattern: int32 [16, 2, 2, 16], P('gx', 'gy'), may hold values 0 or 1
Outputs:
- analysis: float32 [512, 128, 384], P('gx', 'gy')
Inputs may be any that keep to these rules, and one draw needn't show every extreme that they name: `obs_owner`: the tile numbered (its gx index) * 2 + (its gy index). `obs_cell`: cell i * 64 + j of the owner tile, i along the first dimension. `pattern`: 1 where the tile uses the block.
All inputs are finite; a program needn't handle non-finite values. Where the computation divides by a largest or mean magnitude, that divisor is 1e-20 or more.
Results may differ from a plain program's by a relative error of at most 0.0003.
Values sent between devices are 32-bit elements; how exact they have to be, the bound alone decides.
A program may use at most 128 MiB of HBM per device.

v0:
```python
import math

import jax
import jax.numpy as jnp
from jax import lax
from jax.sharding import PartitionSpec as P

ENS = 32
LEV = 4
COMP = 3
NSIT = 4


courant = 0.1
diffusion = 0.08
radius_share = 0.25


def extended_2(shard, sides, width):
    for axis, dim in sides:
        size, length = (lax.axis_size(axis), shard.shape[dim])
        up = [(i, (i + 1) % size) for i in range(size)]
        down = [(j, i) for i, j in up]
        last = lax.slice_in_dim(shard, length - width, length, axis=dim)
        initial = lax.slice_in_dim(shard, 0, width, axis=dim)
        before = lax.ppermute(last, axis, up)
        after = lax.ppermute(initial, axis, down)
        shard = jnp.concatenate([before, shard, after], axis=dim)
    return shard


def update(centre, west_cell, east_cell, south_cell, north_cell):
    speed_east = centre[:, :, 0:1]
    speed_north = centre[:, :, 1:2]
    upwind_flux = (
        jnp.maximum(speed_east, 0.0) * (centre - west_cell)
        + jnp.minimum(speed_east, 0.0) * (east_cell - centre)
        + jnp.maximum(speed_north, 0.0) * (centre - south_cell)
        + jnp.minimum(speed_north, 0.0) * (north_cell - centre)
    )
    return (
        centre
        - courant * upwind_flux
        + diffusion * (west_cell + east_cell + (south_cell + north_cell) - 4.0 * centre)
    )


def interior(extended):
    return update(
        extended[1:-1, 1:-1],
        extended[:-2, 1:-1],
        extended[2:, 1:-1],
        extended[1:-1, :-2],
        extended[1:-1, 2:],
    )


def advance_once(cube_field):
    extended = extended_2(cube_field, (("gx", 0), ("gy", 1)), 1)
    return interior(extended)


def product(left, right):
    return jnp.dot(left, right, precision=lax.Precision.HIGHEST, preferred_element_type=jnp.float32)


def innovations(predicted, obs_value, obs_error):
    centre_obs = jnp.mean(predicted, axis=1, keepdims=True)
    deviation = (predicted - centre_obs) / obs_error[:, None]
    innovation = (obs_value - centre_obs[:, 0]) / obs_error
    return (deviation, innovation)


def localize(
    owners,
    obs_cells,
    block_mask,
    tile_east,
    tile_north,
    span_east,
    span_north,
    tiles_north,
    grid_east,
    grid_north,
):
    place_east = (owners // tiles_north * span_east + obs_cells // span_north).astype(jnp.float32)
    place_north = (owners % tiles_north * span_north + obs_cells % span_north).astype(jnp.float32)
    centre_east = (tile_east * span_east).astype(jnp.float32) + (span_east - 1) / 2.0
    centre_north = (tile_north * span_north).astype(jnp.float32) + (span_north - 1) / 2.0
    gap_east = (
        jnp.remainder(place_east - centre_east + grid_east / 2.0, grid_east) - grid_east / 2.0
    )
    gap_north = (
        jnp.remainder(place_north - centre_north + grid_north / 2.0, grid_north) - grid_north / 2.0
    )
    scale_east = gap_east / (radius_share * grid_east)
    scale_north = gap_north / (radius_share * grid_north)
    weight = jnp.exp(-0.5 * (scale_east * scale_east + scale_north * scale_north))
    blocks = block_mask.shape[0]
    return (weight.reshape(blocks, -1) * block_mask.astype(jnp.float32)[:, None]).reshape(-1)


def transform(deviation, innovation, weight_obs):
    members = deviation.shape[1]
    weighted = deviation * weight_obs[:, None]
    covariance = product(weighted.T, deviation)
    projection = product(weighted.T, innovation[:, None])[:, 0]
    unit_matrix = jnp.eye(members, dtype=jnp.float32)
    system = (members - 1.0) * unit_matrix + covariance
    row_bound = jnp.max(jnp.sum(jnp.abs(system), axis=1))

    def refine(sweep_index, iterates):
        approach, inverse_root = iterates
        middle = 1.5 * unit_matrix - 0.5 * product(inverse_root, approach)
        return (product(approach, middle), product(middle, inverse_root))

    approach, inverse_root = lax.fori_loop(0, NSIT, refine, (system / row_bound, unit_matrix))
    inverse = product(inverse_root, inverse_root) / row_bound
    weights = product(inverse, projection[:, None])[:, 0]
    centring = unit_matrix - 1.0 / members
    shifts = weights[:, None] + math.sqrt(members - 1.0) * inverse_root / jnp.sqrt(row_bound)
    return 1.0 / members + product(centring, shifts)


def local(state, obs_owner, obs_cell, obs_level, obs_coef, obs_value, obs_error, pattern):
    span_east, span_north, features = state.shape
    tiles_east = lax.axis_size("gx")
    tiles_north = lax.axis_size("gy")
    tile_east = lax.axis_index("gx")
    tile_north = lax.axis_index("gy")
    own_tile = tile_east * tiles_north + tile_north
    cube_field = state.reshape(span_east, span_north, COMP, features // COMP)
    for substep in range(2):
        cube_field = advance_once(cube_field)
    flat_rows = cube_field.reshape(-1, ENS)

    def local_prior(table_rows, batch_index):
        owners = obs_owner[batch_index]
        first_row = obs_cell[batch_index] * (COMP * LEV) + obs_level[batch_index]
        obs_coefs = obs_coef[batch_index]
        picked_u = table_rows[first_row]
        picked_v = table_rows[first_row + LEV]
        picked_w = table_rows[first_row + 2 * LEV]
        predicted = (
            obs_coefs[0][:, None] * picked_u
            + obs_coefs[1][:, None] * picked_v
            + obs_coefs[2][:, None] * picked_w
        )
        return jnp.where((owners == own_tile)[:, None], predicted, 0.0)

    def mixing(local_terms, batch_index):
        predicted = lax.psum(local_terms, ("gx", "gy"))
        deviation, innovation = innovations(
            predicted, obs_value[batch_index], obs_error[batch_index]
        )
        weight_obs = localize(
            obs_owner[batch_index],
            obs_cell[batch_index],
            pattern[0, 0, batch_index],
            tile_east,
            tile_north,
            span_east,
            span_north,
            tiles_north,
            span_east * tiles_east,
            span_north * tiles_north,
        )
        return transform(deviation, innovation, weight_obs)

    first_mix = mixing(local_prior(flat_rows, 0), 0)
    flat_rows = product(flat_rows, first_mix)
    second_mix = mixing(local_prior(flat_rows, 1), 1)
    flat_rows = product(flat_rows, second_mix)
    return flat_rows.reshape(span_east, span_north, features)


def solution(mesh):
    placed = (P("gx", "gy", None), P(), P(), P(), P(), P(), P(), P("gx", "gy", None, None))
    return jax.shard_map(
        local, mesh=mesh, in_specs=placed, out_specs=P("gx", "gy", None), check_vma=False
    )
```

profile of v0, /device:TPU:0, one launch (start us, length us, event | category | flops | bytes accessed | tf_op | source)
XLA Modules:
  0.0 580.1 jit_solution(18409301737858495787)
XLA Ops:
  8.3 5.4 collective-permute-start.1
  14.4 5.8 reshape.501
  25.4 8.7 %slice_maximum_fusion.3 = (f32[32,64,1,128]{3,2,1,0:T(1,128)S(1)}, f32[32,64,1,128]{3,2,1,0:T(1,128)S(1)}, f32[32,64,1,128]{3,2,1,0:T(1,128)S(1)}, f32[32,64,1,128]{3,2,1,0:T(1,128)}) fusion(f32[32,64,3,128]{3,2,1,0:T(4,128)} %reshape.501), kind=kLoop, calls=%fused_computation.89 | loop fusion | flops 1048576 | bytes 6291456 | tf_op jit(solution)/shard_map/max | solution.py:36
  45.1 13.6 %fusion.25 = f32[32,64,3,128]{3,2,1,0:T(4,128)S(1)} fusion(f32[1,64,3,128]{3,2,1,0:T(4,128)S(1)} %collective-permute-done.1, f32[32,64,3,128]{3,2,1,0:T(4,128)S(1)} %copy-done, f32[1,64,3,128]{3,2,1,0:T(4,128)S(1)} %collective-permute-done, f32[34,1,3,128]{3,2,1,0:T(4,128)S(1)} %collective-permute-done.3, ...), kind=kLoop, calls=%fused_computation.46 | loop fusion | flops 18874368 | bytes 14129152 | tf_op jit(solution)/shard_map/add | solution.py:42
  58.8 4.4 collective-permute-start.5
  68.0 4.4 slice_maximum_fusion.1
  72.5 9.4 %fusion.11 = f32[32,64,3,128]{3,2,1,0:T(4,128)} fusion(f32[1,64,3,128]{3,2,1,0:T(4,128)S(1)} %collective-permute-done.5, f32[32,64,3,128]{3,2,1,0:T(4,128)S(1)} %fusion.25, f32[1,64,3,128]{3,2,1,0:T(4,128)S(1)} %collective-permute-done.4, f32[34,1,3,128]{3,2,1,0:T(4,128)S(1)} %collective-permute-done.7, f32[34,1,3,128]{3,2,1,0:T(4,128)S(1)} %collective-permute-done.6, ...), kind=kLoop, calls=%fused_computation.28 | loop fusion | flops 22020096 | bytes 10786816 | tf_op jit(solution)/shard_map/add | solution.py:42
  81.9 10.7 %reshape.502 = f32[24576,32]{1,0:T(8,128)} reshape(f32[32,64,3,128]{3,2,1,0:T(4,128)} %fusion.11) | data formatting | bytes 6291456 | tf_op jit(solution)/shard_map/reshape | solution.py:135
  92.6 15.4 %gather_fusion.2 = f32[4096,32]{1,0:T(8,128)S(1)} fusion(f32[24576,32]{1,0:T(8,128)} %reshape.502, s32[4096]{0:T(1024)S(1)} %copy-done.15), kind=kCustom, calls=%fused_computation.2 | custom fusion | bytes 1064960 | tf_op jit(solution)/shard_map/gather | solution.py:143
  108.0 18.8 %gather_fusion.1 = f32[4096,32]{1,0:T(8,128)} fusion(f32[24576,32]{1,0:T(8,128)} %reshape.502, s32[4096]{0:T(1024)S(1)} %copy-done.16), kind=kCustom, calls=%fused_computation.1 | custom fusion | bytes 1064960 | tf_op jit(solution)/shard_map/gather | solution.py:142
  126.8 18.8 %gather_fusion = f32[4096,32]{1,0:T(8,128)} fusion(f32[24576,32]{1,0:T(8,128)} %reshape.502, s32[4096]{0:T(1024)S(1)} %copy-done.14), kind=kCustom, calls=%fused_computation | custom fusion | bytes 1064960 | tf_op jit(solution)/shard_map/gather | solution.py:141
  145.6 7.7 %add_select_fusion.1 = f32[4096,32]{1,0:T(8,128)} fusion(f32[4096,32]{1,0:T(8,128)S(1)} %gather_fusion.2, f32[4096,32]{1,0:T(8,128)} %gather_fusion.1, f32[4096,32]{1,0:T(8,128)} %gather_fusion, f32[4096]{0:T(1024)S(1)} %bitcast.157, f32[4096]{0:T(1024)S(1)} %bitcast.158, f32[4096]{0:T(1024)S(1)} %bitcast.159, pred[4096]{0:T(1024)(128)(4,1)S(1)} %copy-done.21), kind=kLoop, calls=%fused_computation.67 | loop fusion | flops 786432 | bytes 2150400 | tf_op jit(solution)/shard_map/jit(_where)/select_n | solution.py:149
  153.5 133.5 %all-reduce.3.cloned.1.call-done = f32[4096,32]{1,0:T(8,128)} async-done(((f32[4096,32]{1,0:T(8,128)}), f32[4096,32]{1,0:T(8,128)}) %all-reduce.3.cloned.1.call-update) | async-done | bytes 524304 | tf_op jit(solution)/shard_map/psum | solution.py:152
  293.2 4.1 abs_reduce_fusion.1
  304.2 15.8 %fusion.139 = f32[24576,32]{0,1:T(8,128)S(1)} fusion(f32[24576,32]{1,0:T(8,128)} %reshape.502, f32[32,32]{1,0:T(8,128)S(1)} %convolution_add_fusion.1), kind=kOutput, calls=%fused_computation.240 | convolution fusion | flops 301989888 | bytes 6295552 | tf_op jit(solution)/shard_map/dot_general | solution.py:64
  320.0 6.7 %copy.15 = f32[24576,32]{1,0:T(8,128)} copy(f32[24576,32]{0,1:T(8,128)S(1)} %fusion.139) | data formatting | bytes 6291456 | tf_op jit(solution)/shard_map/dot_general | solution.py:64
  326.7 18.8 %gather_fusion.5 = f32[4096,32]{1,0:T(8,128)} fusion(f32[24576,32]{1,0:T(8,128)} %copy.15, s32[4096]{0:T(1024)S(1)} %copy-done.13), kind=kCustom, calls=%fused_computation.5 | custom fusion | bytes 1064960 | tf_op jit(solution)/shard_map/gather | solution.py:143
  345.5 18.8 %gather_fusion.4 = f32[4096,32]{1,0:T(8,128)} fusion(f32[24576,32]{1,0:T(8,128)} %copy.15, s32[4096]{0:T(1024)S(1)} %copy-done.12), kind=kCustom, calls=%fused_computation.4 | custom fusion | bytes 1064960 | tf_op jit(solution)/shard_map/gather | solution.py:142
  364.3 18.8 %gather_fusion.3 = f32[4096,32]{1,0:T(8,128)} fusion(f32[24576,32]{1,0:T(8,128)} %copy.15, s32[4096]{0:T(1024)S(1)} %copy-done.11), kind=kCustom, calls=%fused_computation.3 | custom fusion | bytes 1064960 | tf_op jit(solution)/shard_map/gather | solution.py:141
  383.0 7.7 %add_select_fusion = f32[4096,32]{1,0:T(8,128)} fusion(f32[4096,32]{1,0:T(8,128)} %gather_fusion.5, f32[4096,32]{1,0:T(8,128)} %gather_fusion.4, f32[4096,32]{1,0:T(8,128)} %gather_fusion.3, f32[4096]{0:T(1024)S(1)} %bitcast.155, f32[4096]{0:T(1024)S(1)} %bitcast.156, f32[4096]{0:T(1024)S(1)} %bitcast.154, pred[4096]{0:T(1024)(128)(4,1)S(1)} %broadcast_compare_fusion), kind=kLoop, calls=%fused_computation.65 | loop fusion | flops 786432 | bytes 2150400 | tf_op jit(solution)/shard_map/jit(_where)/select_n | solution.py:149
  390.9 132.7 %all-reduce.5.cloned.1.call-done = f32[4096,32]{1,0:T(8,128)} async-done(((f32[4096,32]{1,0:T(8,128)}), f32[4096,32]{1,0:T(8,128)}) %all-reduce.5.cloned.1.call-update) | async-done | bytes 524304 | tf_op jit(solution)/shard_map/psum | solution.py:152
  529.9 4.1 abs_reduce_fusion
  540.8 22.4 %fusion.140 = f32[24576,32]{1,0:T(8,128)} fusion(f32[24576,32]{0,1:T(8,128)S(1)} %fusion.139, f32[32,32]{1,0:T(8,128)S(1)} %convolution_add_fusion), kind=kOutput, calls=%fused_computation.241 | convolution fusion | flops 301989888 | bytes 6295552 | tf_op jit(solution)/shard_map/dot_general | solution.py:64
  563.2 9.7 %reshape.503 = f32[32,64,384]{2,1,0:T(8,128)} reshape(f32[24576,32]{1,0:T(8,128)} %fusion.140) | data formatting | bytes 6291456 | tf_op jit(solution)/shard_map/reshape | solution.py:174
  (157 shorter events, 52.7 us)
Async XLA Ops:
  6.5 13.6 %copy-start.17 = (s32[2,4096]{1,0:T(2,128)S(1)}, s32[2,4096]{1,0:T(2,128)}, u32[]{:S(2)}) copy-start(s32[2,4096]{1,0:T(2,128)} %param.13) | copy-start | bytes 98308
  6.5 13.7 %copy-start.18 = (f32[2,4096]{1,0:T(2,128)S(1)}, f32[2,4096]{1,0:T(2,128)}, u32[]{:S(2)}) copy-start(f32[2,4096]{1,0:T(2,128)} %param.17) | copy-start | bytes 98308
  6.5 14.3 %copy-start.19 = (f32[2,4096]{1,0:T(2,128)S(1)}, f32[2,4096]{1,0:T(2,128)}, u32[]{:S(2)}) copy-start(f32[2,4096]{1,0:T(2,128)} %param.18) | copy-start | bytes 98308
  6.5 14.4 %copy-start.2 = (s32[2,4096]{1,0:T(2,128)S(1)}, s32[2,4096]{1,0:T(2,128)}, u32[]{:S(2)}) copy-start(s32[2,4096]{1,0:T(2,128)} %param.14) | copy-start | bytes 98308
  6.5 15.0 %copy-start.20 = (s32[2,4096]{1,0:T(2,128)S(1)}, s32[2,4096]{1,0:T(2,128)}, u32[]{:S(2)}) copy-start(s32[2,4096]{1,0:T(2,128)} %param.15) | copy-start | bytes 98308
  6.6 280.5 %all-reduce.3.cloned.1.call-start = ((), (), s32[]{:S(2)}) async-start(), calls=%async_computation | async-start | bytes 4194304 | tf_op jit(solution)/shard_map/psum | solution.py:152
  7.6 17.1 %copy-start.3 = (f32[2,3,4096]{2,0,1:T(2,128)S(1)}, f32[2,3,4096]{2,0,1:T(2,128)}, u32[]{:S(2)}) copy-start(f32[2,3,4096]{2,0,1:T(2,128)} %param.16) | copy-start | bytes 294916
  8.3 30.9 %collective-permute-start.1 = (f32[1,64,3,128]{3,2,1,0:T(4,128)}, f32[1,64,3,128]{3,2,1,0:T(4,128)S(1)}, u32[]{:S(2)}, u32[]{:S(2)}) collective-permute-start(f32[1,64,3,128]{3,2,1,0:T(4,128)} %slice.151), channel_id=1, source_target_pairs={{2,0},{4,2},{6,4},{8,6},{10,8},{12,10},{14,12},{16,14},{18,16},{20... | collective-permute-start | bytes 294920 | tf_op jit(solution)/shard_map/ppermute | solution.py:27
  14.4 20.9 %collective-permute-start = (f32[1,64,3,128]{3,2,1,0:T(4,128)}, f32[1,64,3,128]{3,2,1,0:T(4,128)S(1)}, u32[]{:S(2)}, u32[]{:S(2)}) collective-permute-start(f32[1,64,3,128]{3,2,1,0:T(4,128)} %slice.148), channel_id=1, source_target_pairs={{0,2},{2,4},{4,6},{6,8},{8,10},{10,12},{12,14},{14,16},{16,18},{18... | collective-permute-start | bytes 294920 | tf_op jit(solution)/shard_map/ppermute | solution.py:26
  39.2 4.4 collective-permute-start.2
  40.8 4.3 collective-permute-start.3
  58.8 7.1 %collective-permute-start.4 = (f32[1,64,3,128]{3,2,1,0:T(4,128)S(1)}, f32[1,64,3,128]{3,2,1,0:T(4,128)S(1)}, u32[]{:S(2)}, u32[]{:S(2)}) collective-permute-start(f32[1,64,3,128]{3,2,1,0:T(4,128)S(1)} %get-tuple-element.103), channel_id=1, source_target_pairs={{0,2},{2,4},{4,6},{6,8},{8,10},{10,12},{12,14},{14,16},{16,18},{18... | collective-permute-start | bytes 294920 | tf_op jit(solution)/shard_map/ppermute | solution.py:26
  58.8 7.1 %collective-permute-start.5 = (f32[1,64,3,128]{3,2,1,0:T(4,128)S(1)}, f32[1,64,3,128]{3,2,1,0:T(4,128)S(1)}, u32[]{:S(2)}, u32[]{:S(2)}) collective-permute-start(f32[1,64,3,128]{3,2,1,0:T(4,128)S(1)} %get-tuple-element.104), channel_id=1, source_target_pairs={{2,0},{4,2},{6,4},{8,6},{10,8},{12,10},{14,12},{16,14},{18,16},{20... | collective-permute-start | bytes 294920 | tf_op jit(solution)/shard_map/ppermute | solution.py:27
  65.9 6.5 %collective-permute-start.6 = (f32[34,1,3,128]{3,2,1,0:T(4,128)S(1)}, f32[34,1,3,128]{3,2,1,0:T(4,128)S(1)}, u32[]{:S(2)}, u32[]{:S(2)}) collective-permute-start(f32[34,1,3,128]{3,2,1,0:T(4,128)S(1)} %get-tuple-element.95), channel_id=1, source_target_pairs={{0,1},{1,0},{2,3},{3,2},{4,5},{5,4},{6,7},{7,6},{8,9},{9,8},{10,11... | collective-permute-start | bytes 156680 | tf_op jit(solution)/shard_map/ppermute | solution.py:26
  66.8 5.7 collective-permute-start.7
  92.6 15.4 %copy-start.16 = (s32[4096]{0:T(1024)S(1)}, s32[4096]{0:T(1024)}, u32[]{:S(2)}) copy-start(s32[4096]{0:T(1024)} %broadcast_clamp_fusion.4) | copy-start | bytes 49156
  108.0 18.8 %copy-start.14 = (s32[4096]{0:T(1024)S(1)}, s32[4096]{0:T(1024)}, u32[]{:S(2)}) copy-start(s32[4096]{0:T(1024)} %broadcast_clamp_fusion.5) | copy-start | bytes 49156
  126.8 18.8 %copy-start.4 = (f32[1,1,4096]{2,0,1:T(1,128)S(1)}, f32[1,1,4096]{2,0,1:T(1,128)}, u32[]{:S(2)}) copy-start(f32[1,1,4096]{2,0,1:T(1,128)} %get-tuple-element.114) | copy-start | bytes 49156
  126.8 18.8 %copy-start.21 = (pred[4096]{0:T(1024)(128)(4,1)S(1)}, pred[4096]{0:T(1024)(128)(4,1)}, u32[]{:S(2)}) copy-start(pred[4096]{0:T(1024)(128)(4,1)} %broadcast_compare_fusion.1) | copy-start | bytes 12292
  153.2 136.0 %copy-start.7 = (f32[1,4096]{1,0:T(1,128)S(1)}, f32[1,4096]{1,0:T(1,128)}, u32[]{:S(2)}) copy-start(f32[1,4096]{1,0:T(1,128)} %get-tuple-element.120) | copy-start | bytes 49156
  153.2 370.4 %all-reduce.5.cloned.1.call-start = ((), (), s32[]{:S(2)}) async-start(), calls=%async_computation.1 | async-start | bytes 4194304 | tf_op jit(solution)/shard_map/psum | solution.py:152
  326.7 18.8 %copy-start.12 = (s32[4096]{0:T(1024)S(1)}, s32[4096]{0:T(1024)}, u32[]{:S(2)}) copy-start(s32[4096]{0:T(1024)} %broadcast_clamp_fusion.1) | copy-start | bytes 49156
  345.5 18.8 %copy-start.11 = (s32[4096]{0:T(1024)S(1)}, s32[4096]{0:T(1024)}, u32[]{:S(2)}) copy-start(s32[4096]{0:T(1024)} %broadcast_clamp_fusion.2) | copy-start | bytes 49156
  390.8 135.1 %copy-start.5 = (f32[1,4096]{1,0:T(1,128)S(1)}, f32[1,4096]{1,0:T(1,128)}, u32[]{:S(2)}) copy-start(f32[1,4096]{1,0:T(1,128)} %get-tuple-element.119) | copy-start | bytes 49156
  (9 other events, 81.9 us)
Sparse Core Ops, SparseCore 0:
  153.4 133.6 all-reduce.2
  390.9 132.6 all-reduce.4
where the time goes:
time: 590 us; the launch traced here: 580 us
  waiting for transfers between devices  272 us (46%)
  local copies, waits for them, and re-layouts  151 us (26%)
  other arithmetic  70.9 us (12%)
  matrix products  55.6 us (9%)
  between operations  15.7 us (3%)
  starting transfers between devices  14.2 us (2%)
    psum x2, waiting for transfers between devices, mixing(): predicted = lax.psum(local_terms, ('gx', 'gy'))  266 us
    dot_general x36, matrix products, product(): jnp.dot(left, right, precision=lax.Precision.HIGHEST, preferred_element_t...  55.6 us
    gather x2, local copies, waits for them, and re-layouts, local_prior(): picked_v = table_rows[first_row + LEV]  37.5 us
    gather x2, local copies, waits for them, and re-layouts, local_prior(): picked_u = table_rows[first_row]  37.5 us
    gather x2, local copies, waits for them, and re-layouts, local_prior(): picked_w = table_rows[first_row + 2 * LEV]  34.1 us
    add x2, other arithmetic, update(): centre - courant * upwind_flux  23 us
    select_n x2, other arithmetic, local_prior(): return jnp.where((owners == own_tile)[:, None], predicted, 0.0)  15.4 us
    max x2, other arithmetic, update(): jnp.maximum(speed_east, 0.0) * (centre - west_cell)  13.1 us
  transfers between devices with their start and end apart: 10, of which 5 were waited for; matrix products, arithmetic and copies ran while one was open for 5% of the time, Pallas kernels for 0%

commit v1 on v0

v1 whole, which is shorter than its diff:
```python
import functools
import math

import jax
import jax.numpy as jnp
from jax import lax
from jax.experimental import pallas as pl
from jax.experimental.pallas import tpu as pltpu
from jax.sharding import PartitionSpec as P

ENS = 32
LEV = 4
COMP = 3
NSIT = 4
CHUNK = 256
LANES = 128

courant = 0.1
diffusion = 0.08
radius_share = 0.25

VMEM_LIMIT = 48 * 1024 * 1024
HIGHEST = lax.Precision.HIGHEST
F32 = jnp.float32
BF16 = jnp.bfloat16

smem = pl.BlockSpec(memory_space=pltpu.SMEM)
vmem = pl.BlockSpec(memory_space=pltpu.VMEM)


def exact_dot(left, right):
    return jnp.dot(left, right, precision=HIGHEST, preferred_element_type=F32)


def half_dot(left, right):
    return jnp.dot(left, right, preferred_element_type=F32)


def split(values):
    high = values.astype(BF16)
    low = (values - high.astype(F32)).astype(BF16)
    return high, low


def compact_kernel(nobs, tile_ref, owner_ref, order_ref, count_ref):
    me = tile_ref[0]
    step = 16
    for batch in range(2):
        base = batch * nobs

        def body(i, count):
            first = i * step
            owners = [owner_ref[base + first + k] for k in range(step)]
            for k in range(step):
                order_ref[base + count] = first + k
                count = count + jnp.where(owners[k] == me, 1, 0)
            return count

        count_ref[batch] = lax.fori_loop(0, nobs // step, body, 0)


def compact(tile, owners):
    batches, nobs = owners.shape
    return pl.pallas_call(
        functools.partial(compact_kernel, nobs),
        out_shape=(
            jax.ShapeDtypeStruct((batches * nobs,), jnp.int32),
            jax.ShapeDtypeStruct((batches,), jnp.int32),
        ),
        in_specs=[smem, smem],
        out_specs=(smem, smem),
        cost_estimate=pl.CostEstimate(flops=40_000_000, bytes_accessed=20_000_000, transcendentals=0),
    )(tile, owners.reshape(-1))


def forecast_kernel(state_ref, west_ref, east_ref, south_ref, north_ref, out_ref, wide, middle):
    nx, ny, _ = state_ref.shape
    wide[2 : nx + 2, 8 : ny + 8, :] = state_ref[...]
    wide[0:2, 8 : ny + 8, :] = west_ref[...]
    wide[nx + 2 : nx + 4, 8 : ny + 8, :] = east_ref[...]
    wide[:, 6:8, :] = south_ref[...]
    wide[:, ny + 8 : ny + 10, :] = north_ref[...]
    rows = ny + 16

    def updated(src, x, comp, up, um, vp, vm):
        lanes = slice(comp * LANES, (comp + 1) * LANES)
        centre = src[x, :, lanes]
        west = src[x - 1, :, lanes]
        east = src[x + 1, :, lanes]
        south = pltpu.roll(centre, 1, 0)
        north = pltpu.roll(centre, rows - 1, 0)
        flux = up * (centre - west) + um * (east - centre) + vp * (centre - south) + vm * (north - centre)
        return centre - courant * flux + diffusion * ((west + east) + (south + north) - 4.0 * centre)

    def speeds(src, x):
        u = src[x, :, 0:LANES]
        v = src[x, :, LANES : 2 * LANES]
        return jnp.maximum(u, 0.0), jnp.minimum(u, 0.0), jnp.maximum(v, 0.0), jnp.minimum(v, 0.0)

    def first(i, carry):
        parts = speeds(wide, i + 1)
        for comp in range(COMP):
            middle[i, :, comp * LANES : (comp + 1) * LANES] = updated(wide, i + 1, comp, *parts)
        return carry

    lax.fori_loop(0, nx + 2, first, 0)

    def second(i, carry):
        parts = speeds(middle, i + 1)
        for comp in range(COMP):
            new = updated(middle, i + 1, comp, *parts)
            out_ref[pl.ds(pl.multiple_of(i * ny, ny), ny), comp * LANES : (comp + 1) * LANES] = new[8 : ny + 8]
        return carry

    lax.fori_loop(0, nx, second, 0)


def forecast(state, west, east, south, north):
    nx, ny, feat = state.shape
    return pl.pallas_call(
        forecast_kernel,
        out_shape=jax.ShapeDtypeStruct((nx * ny, feat), F32),
        in_specs=[vmem] * 5,
        out_specs=vmem,
        scratch_shapes=[
            pltpu.VMEM((nx + 4, ny + 16, feat), F32),
            pltpu.VMEM((nx + 2, ny + 16, feat), F32),
        ],
        compiler_params=pltpu.CompilerParams(vmem_limit_bytes=VMEM_LIMIT),
    )(state, west, east, south, north)


def sums_kernel(batch, nobs, tiles, mixed, count_ref, order_ref, cell_ref, field_ref, table_ref, *rest):
    if mixed:
        mix_ref, out_ref, picked, params, total = rest
    else:
        out_ref, picked, params, total = rest
    count = count_ref[batch]
    base = batch * nobs
    total[...] = jnp.zeros_like(total)
    lane = lax.broadcasted_iota(jnp.int32, (CHUNK, LANES), 1)
    group = lane // ENS
    row = lax.broadcasted_iota(jnp.int32, (CHUNK, 1), 0)
    width = table_ref.shape[1] - LANES
    tile_of_row = lax.broadcasted_iota(jnp.int32, (width, 256), 0)
    tile_of_lane = lax.broadcasted_iota(jnp.int32, (width, 256), 1) // ENS

    def chunk(ci, carry):
        def pick(i, carry):
            for k in range(8):
                at = i * 8 + k
                place = ci * CHUNK + at
                j = jnp.where(place < count, order_ref[base + place], 0)
                picked[pl.ds(at, 1), :] = field_ref[pl.ds(cell_ref[base + j], 1), :]
                params[pl.ds(at, 1), :] = table_ref[pl.ds(j, 1), :]
            return carry

        lax.fori_loop(0, CHUNK // 8, pick, 0)
        param = params[:, 0:LANES]
        values = (
            param[:, 0:1] * picked[:, 0:LANES]
            + param[:, 1:2] * picked[:, LANES : 2 * LANES]
            + param[:, 2:3] * picked[:, 2 * LANES : 3 * LANES]
        )
        values = jnp.where(group.astype(F32) == param[:, 3:4], values, 0.0)
        values = values + pltpu.roll(values, 64, 1)
        values = values + pltpu.roll(values, 32, 1)
        if mixed:
            values = exact_dot(values, mix_ref[...])
        centre = jnp.sum(values, axis=1, keepdims=True) / float(LANES)
        inverse_error = param[:, 5:6]
        deviation = (values - centre) * inverse_error
        innovation = (param[:, 4:5] - centre) * inverse_error
        rho = jnp.where(ci * CHUNK + row < count, params[:, LANES:], 0.0)
        left = jnp.where(group == 0, deviation, jnp.where(lane == ENS, innovation, 0.0))
        high, low = split(left.T[0:48])
        both = jnp.concatenate([high, low], axis=0)
        rho_high, rho_low = split(rho)
        pair = jnp.concatenate([deviation, deviation], axis=1)
        for g in range(tiles // 8):
            spread = jnp.where(tile_of_row == tile_of_lane + g * 8, 1.0, 0.0).astype(BF16)
            weight = half_dot(rho_high, spread) + half_dot(rho_low, spread)
            right_high, right_low = split(weight * pair)
            first = half_dot(both, right_high)
            second = half_dot(high, right_low)
            total[:, g * 256 : (g + 1) * 256] += first[0:48] + first[48:96] + second
        return carry

    lax.fori_loop(0, (count + CHUNK - 1) // CHUNK, chunk, 0)
    small = lax.broadcasted_iota(jnp.int32, (8, LANES), 1) // ENS

    def pack(q, carry):
        lanes = pl.ds(pl.multiple_of(q * LANES, LANES), LANES)
        blocks = [total[8 * r : 8 * r + 8, lanes] for r in range(5)]
        for t in range(4):
            packed = jnp.zeros((8, LANES), F32)
            for r in range(4):
                moved = pltpu.roll(blocks[r], (32 * (r - t)) % LANES, 1) if r != t else blocks[r]
                packed = jnp.where(small == r, moved, packed)
            proj = pltpu.roll(blocks[4], (-32 * t) % LANES, 1) if t else blocks[4]
            out_ref[q * 4 + t, 0:8, :] = packed
            out_ref[q * 4 + t, 8:16, :] = jnp.where(small == 0, proj, 0.0)
        return carry

    lax.fori_loop(0, tiles // 4, pack, 0)


def own_sums(batch, nobs, tiles, counts, order, cells, field, table, mix=None):
    extra = [] if mix is None else [mix]
    return pl.pallas_call(
        functools.partial(sums_kernel, batch, nobs, tiles, mix is not None),
        out_shape=jax.ShapeDtypeStruct((tiles, 16, LANES), F32),
        in_specs=[smem] * 3 + [vmem] * (2 + len(extra)),
        out_specs=vmem,
        scratch_shapes=[
            pltpu.VMEM((CHUNK, COMP * LANES), F32),
            pltpu.VMEM((CHUNK, table.shape[1]), F32),
            pltpu.VMEM((48, tiles * ENS), F32),
        ],
        compiler_params=pltpu.CompilerParams(vmem_limit_bytes=VMEM_LIMIT),
    )(counts, order, cells, field, table, *extra)


def mix_kernel(tiles_east, tiles_north, x_ref, out_ref, held, send_sem, recv_sem):
    tiles = tiles_east * tiles_north
    me = lax.axis_index("gx") * tiles_north + lax.axis_index("gy")

    def device(t):
        return (t // tiles_north, lax.rem(t, tiles_north))

    barrier = pltpu.get_barrier_semaphore()

    def greet(d, carry):
        pl.semaphore_signal(
            barrier, inc=1, device_id=device(lax.rem(me + d, tiles)), device_id_type=pl.DeviceIdType.MESH
        )
        return carry

    lax.fori_loop(1, tiles, greet, 0)
    pl.semaphore_wait(barrier, tiles - 1)

    def send(d, carry):
        target = lax.rem(me + d, tiles)
        pltpu.make_async_remote_copy(
            src_ref=x_ref.at[target],
            dst_ref=held.at[d - 1],
            send_sem=send_sem,
            recv_sem=recv_sem,
            device_id=device(target),
            device_id_type=pl.DeviceIdType.MESH,
        ).start()
        return carry

    lax.fori_loop(1, tiles, send, 0)
    pltpu.make_async_copy(held, held, recv_sem).wait()
    pltpu.make_async_copy(held, held, send_sem).wait()

    total = lax.fori_loop(0, tiles - 1, lambda d, acc: acc + held[d], x_ref[me])
    top = total[0:8]
    cov = jnp.concatenate([top] + [pltpu.roll(top, LANES - 32 * r, 1) for r in range(1, 4)], axis=0)[:, 0:ENS]
    proj = total[8:9, 0:ENS]
    ri = lax.broadcasted_iota(jnp.int32, (ENS, ENS), 0)
    ci = lax.broadcasted_iota(jnp.int32, (ENS, ENS), 1)
    unit = jnp.where(ri == ci, 1.0, 0.0)
    system = (ENS - 1.0) * unit + cov
    bound = jnp.max(jnp.sum(jnp.abs(system), axis=1, keepdims=True), axis=0, keepdims=True)
    approach, root = system / bound, unit
    for sweep in range(NSIT):
        middle = 1.5 * unit - 0.5 * exact_dot(root, approach)
        approach, root = exact_dot(approach, middle), exact_dot(middle, root)
    inverse = exact_dot(root, root) / bound
    weights = jnp.sum(inverse * proj, axis=1, keepdims=True)
    shifts = weights + math.sqrt(ENS - 1.0) * root / jnp.sqrt(bound)
    mix = 1.0 / ENS + (shifts - jnp.mean(shifts, axis=0, keepdims=True))
    er = lax.broadcasted_iota(jnp.int32, (ENS, LANES), 0)
    ec = lax.broadcasted_iota(jnp.int32, (ENS, LANES), 1)
    repeated = exact_dot(mix, jnp.where(lax.rem(ec, ENS) == er, 1.0, 0.0))
    full = jnp.concatenate([repeated] * 4, axis=0)
    br = lax.broadcasted_iota(jnp.int32, (LANES, LANES), 0) // ENS
    bc = lax.broadcasted_iota(jnp.int32, (LANES, LANES), 1) // ENS
    out_ref[...] = jnp.where(br == bc, full, 0.0)


def tile_mix(tiles_east, tiles_north, sums):
    tiles = tiles_east * tiles_north
    return pl.pallas_call(
        functools.partial(mix_kernel, tiles_east, tiles_north),
        out_shape=jax.ShapeDtypeStruct((LANES, LANES), F32),
        in_specs=[vmem],
        out_specs=vmem,
        scratch_shapes=[
            pltpu.VMEM((tiles - 1, 16, LANES), F32),
            pltpu.SemaphoreType.DMA,
            pltpu.SemaphoreType.DMA,
        ],
        compiler_params=pltpu.CompilerParams(
            collective_id=0, has_side_effects=True, vmem_limit_bytes=VMEM_LIMIT
        ),
    )(sums)


def apply_kernel(field_ref, one_ref, two_ref, out_ref):
    high, low = split(exact_dot(one_ref[...], two_ref[...]))
    for comp in range(COMP):
        lanes = slice(comp * LANES, (comp + 1) * LANES)
        value_high, value_low = split(field_ref[:, lanes])
        out_ref[:, lanes] = half_dot(value_high, high) + half_dot(value_low, high) + half_dot(value_high, low)


def apply_mix(field, one, two):
    rows, feat = field.shape
    block = 512
    return pl.pallas_call(
        apply_kernel,
        out_shape=jax.ShapeDtypeStruct((rows, feat), F32),
        grid=(rows // block,),
        in_specs=[
            pl.BlockSpec((block, feat), lambda i: (i, 0)),
            pl.BlockSpec((LANES, LANES), lambda i: (0, 0)),
            pl.BlockSpec((LANES, LANES), lambda i: (0, 0)),
        ],
        out_specs=pl.BlockSpec((block, feat), lambda i: (i, 0)),
        compiler_params=pltpu.CompilerParams(vmem_limit_bytes=VMEM_LIMIT),
    )(field, one, two)


def neighbours(axis, last, initial):
    size = lax.axis_size(axis)
    up = [(i, (i + 1) % size) for i in range(size)]
    down = [(j, i) for i, j in up]
    return lax.ppermute(last, axis, up), lax.ppermute(initial, axis, down)


def distance_weights(owners, cells, span_east, span_north, tiles_east, tiles_north):
    grid_east, grid_north = span_east * tiles_east, span_north * tiles_north
    place_east = (owners // tiles_north * span_east + cells // span_north).astype(F32)[:, None]
    place_north = (owners % tiles_north * span_north + cells % span_north).astype(F32)[:, None]
    tile = jnp.arange(tiles_east * tiles_north, dtype=jnp.int32)[None, :]
    centre_east = (tile // tiles_north * span_east).astype(F32) + (span_east - 1) / 2.0
    centre_north = (tile % tiles_north * span_north).astype(F32) + (span_north - 1) / 2.0
    gap_east = place_east - centre_east
    gap_east = jnp.where(gap_east >= grid_east / 2.0, gap_east - grid_east, gap_east)
    gap_east = jnp.where(gap_east < -grid_east / 2.0, gap_east + grid_east, gap_east)
    gap_north = place_north - centre_north
    gap_north = jnp.where(gap_north >= grid_north / 2.0, gap_north - grid_north, gap_north)
    gap_north = jnp.where(gap_north < -grid_north / 2.0, gap_north + grid_north, gap_north)
    scale_east = gap_east / (radius_share * grid_east)
    scale_north = gap_north / (radius_share * grid_north)
    return jnp.exp(-0.5 * (scale_east * scale_east + scale_north * scale_north))


def local(state, obs_owner, obs_cell, obs_level, obs_coef, obs_value, obs_error, pattern):
    span_east, span_north, features = state.shape
    tiles_east = lax.axis_size("gx")
    tiles_north = lax.axis_size("gy")
    tiles = tiles_east * tiles_north
    own_tile = lax.axis_index("gx") * tiles_north + lax.axis_index("gy")
    nobs = obs_owner.shape[1]

    west, east = neighbours("gx", state[-2:], state[:2])
    last = jnp.concatenate([west[:, -2:], state[:, -2:], east[:, -2:]], axis=0)
    initial = jnp.concatenate([west[:, :2], state[:, :2], east[:, :2]], axis=0)
    south, north = neighbours("gy", last, initial)

    patterns = lax.all_gather(pattern[0, 0], ("gx", "gy"))
    order, counts = compact(jnp.reshape(own_tile, (1,)).astype(jnp.int32), obs_owner)
    cells = obs_cell.reshape(-1)
    width = -(-tiles // LANES) * LANES
    tables = []
    for batch in range(2):
        blocks = patterns.shape[2]
        rho = distance_weights(
            obs_owner[batch], obs_cell[batch], span_east, span_north, tiles_east, tiles_north
        ).reshape(blocks, nobs // blocks, tiles)
        rho = (rho * patterns[:, batch].T.astype(F32)[:, None, :]).reshape(nobs, tiles)
        columns = jnp.stack(
            [
                obs_coef[batch, 0],
                obs_coef[batch, 1],
                obs_coef[batch, 2],
                obs_level[batch].astype(F32),
                obs_value[batch],
                1.0 / obs_error[batch],
            ],
            axis=1,
        )
        tables.append(
            jnp.concatenate(
                [
                    jnp.pad(columns, ((0, 0), (0, LANES - columns.shape[1]))),
                    jnp.pad(rho, ((0, 0), (0, width - tiles))),
                ],
                axis=1,
            )
        )

    field = forecast(state, west, east, south, north)
    sums = own_sums(0, nobs, tiles, counts, order, cells, field, tables[0])
    first_mix = tile_mix(tiles_east, tiles_north, sums)
    sums = own_sums(1, nobs, tiles, counts, order, cells, field, tables[1], first_mix)
    second_mix = tile_mix(tiles_east, tiles_north, sums)
    return apply_mix(field, first_mix, second_mix).reshape(span_east, span_north, features)


def solution(mesh):
    placed = (P("gx", "gy", None), P(), P(), P(), P(), P(), P(), P("gx", "gy", None, None))
    return jax.shard_map(
        local, mesh=mesh, in_specs=placed, out_specs=P("gx", "gy", None), check_vma=False
    )
```

time: 590 us -> 182 us (0.31); the launches traced: 580 us -> 180 us
  waiting for transfers between devices: 272 us -> 0.01 us
  local copies, waits for them, and re-layouts: 151 us -> 7.8 us
  Pallas kernels: 0 us -> 90.4 us
  blocking collectives: 0 us -> 65.3 us
  other arithmetic: 70.9 us -> 8.82 us
  matrix products: 55.6 us -> 0 us
  between operations: 15.7 us -> 0.27 us
  starting transfers between devices: 14.2 us -> 7.69 us
    psum x2 -> x0, waiting for transfers between devices: 266 us -> none  [mixing(): predicted = lax.psum(local_terms, ('gx', 'gy'))]
    gather x6 -> x0, local copies, waits for them, and re-layouts: 109 us -> none  [the longest x2 37.5 us: local_prior(): picked_v = table_rows[first_row + LEV]]
    pallas_call x0 -> x7, Pallas kernels: none -> 90.4 us  [the longest x2 37.7 us: tile_mix(): pl.pallas_call(functools.partial(mix_kernel, tiles_east, tiles_north), ou...]
    all_gather x0 -> x1, blocking collectives: none -> 65.3 us  [local(): patterns = lax.all_gather(pattern[0, 0], ('gx', 'gy'))]
    dot_general x36 -> x0, matrix products: 55.6 us -> none  [product(): jnp.dot(left, right, precision=lax.Precision.HIGHEST, preferred_element_t...]
    reshape x3 -> x0, local copies, waits for them, and re-layouts: 26.1 us -> none  [the longest x1 10.7 us: local(): flat_rows = cube_field.reshape(-1, ENS)]
    add x2, other arithmetic: 23 us -> 0.01 us  [the longest x1 0.01 us: distance_weights(): (tile % tiles_north * span_north).astype(F32) + (span_north - 1) / 2.0]
    select_n x4 -> x0, other arithmetic: 15.5 us -> none  [the longest x2 15.4 us: local_prior(): return jnp.where((owners == own_tile)[:, None], predicted, 0.0)]
  transfers between devices with their start and end apart: 10 -> 4, of which waited for: 5 -> 0; matrix products, arithmetic and copies ran while one was open for 5% -> 9% of each run, Pallas kernels for 0% -> 15%
where the time goes in v1:
time: 182 us; the launch traced here: 180 us
  Pallas kernels  90.4 us (50%)
  blocking collectives  65.3 us (36%)
  other arithmetic  8.82 us (5%)
  local copies, waits for them, and re-layouts  7.8 us (4%)
  starting transfers between devices  7.69 us (4%)
    all_gather x1, blocking collectives, local(): patterns = lax.all_gather(pattern[0, 0], ('gx', 'gy'))  65.3 us
    pallas_call x2, Pallas kernels, tile_mix(): pl.pallas_call(functools.partial(mix_kernel, tiles_east, tiles_north), ou...  37.7 us
    pallas_call x1, Pallas kernels, compact(): pl.pallas_call(functools.partial(compact_kernel, nobs), out_shape=(jax.Sh...  26.6 us
    pallas_call x2, Pallas kernels, own_sums(): pl.pallas_call(functools.partial(sums_kernel, batch, nobs, tiles, mix is...  13.4 us
    pallas_call x1, Pallas kernels, forecast(): pl.pallas_call(forecast_kernel, out_shape=jax.ShapeDtypeStruct((nx * ny,...  8.72 us
    ppermute x4, starting transfers between devices, neighbours(): return (lax.ppermute(last, axis, up), lax.ppermute(initial, axis, down))  7.69 us
    another operation x6, local copies, waits for them, and re-layouts, local(): jnp.stack([obs_coef[batch, 0], obs_coef[batch, 1], obs_coef[batch, 2], ob...  4.71 us
    pallas_call x1, Pallas kernels, apply_mix(): pl.pallas_call(apply_kernel, out_shape=jax.ShapeDtypeStruct((rows, feat),...  3.99 us
  transfers between devices with their start and end apart: 4, of which 0 were waited for; matrix products, arithmetic and copies ran while one was open for 9% of the time, Pallas kernels for 15%

profile of v1, /device:TPU:0, one launch (start us, length us, event | category | flops | bytes accessed | tf_op | source)
XLA Modules:
  0.0 180.3 jit_solution(14314412707301895283)
XLA Ops:
  0.0 1.0 fusion.43
  1.1 0.5 collective-permute-start
  1.6 5.0 %collective-permute-start.1 = (f32[2,64,384]{2,1,0:T(8,128)S(1)}, f32[2,64,384]{2,1,0:T(8,128)S(1)}, u32[]{:S(2)}, u32[]{:S(2)}) collective-permute-start(f32[2,64,384]{2,1,0:T(8,128)S(1)} %get-tuple-element.11), channel_id=1, source_target_pairs={{2,0},{4,2},{6,4},{8,6},{10,8},{12,10},{14,12},{16,14},{18,16},{20... | collective-permute-start | bytes 589832 | tf_op jit(solution)/shard_map/ppermute | solution.py:331
  6.6 1.0 slice_bitcast_fusion.1
  7.6 0.9 divide_bitcast_fusion
  8.4 0.9 slice_bitcast_fusion
  9.3 0.9 convert_bitcast_fusion
  10.2 0.2 stack.4
  10.4 0.6 copy.25
  11.2 2.0 %copy.27 = f32[4096,6]{1,0:T(8,128)} copy(f32[4096,6]{0,1:T(8,128)S(1)} %stack.5) | data formatting | bytes 196608 | tf_op jit(solution)/shard_map/stack | solution.py:376
  13.2 65.3 %all-gather = s32[32,1,2,16]{3,2,1,0:T(2,128)S(1)} all-gather(s32[1,1,2,16]{3,2,1,0:T(2,128)S(1)} %copy-done.5), channel_id=2, replica_groups=mesh['gx'=16,'gy'=2] {'gx','gy'}, dimensions={0}, use_global_device_ids=true | all-gather | bytes 4224 | tf_op jit(solution)/shard_map/all_gather | solution.py:365
  78.8 3.3 %fusion.13 = (f32[4096,32]{1,0:T(8,128)S(1)}, f32[4096,32]{1,0:T(8,128)S(1)}) fusion(f32[16,32]{1,0:T(8,128)S(1)} %copy.28, f32[4096]{0:T(1024)S(1)} %get-tuple-element.30, f32[4096]{0:T(1024)S(1)} %get-tuple-element.29, f32[32]{0:T(128)S(1)} %fusion.38, f32[32]{0:T(128)S(1)} %fusion.41, f32[16,32]{1,0:T(8,128)S(1)} %copy.26, ...), kind=kLoop, calls=%fused_computation.25 | loop fusion | flops 5505024 | bytes 1118464 | tf_op jit(solution)/shard_map/mul | solution.py:375
  82.1 1.2 fusion.42
  83.4 0.4 collective-permute-start.3
  83.9 1.7 collective-permute-start.2
  85.6 3.6 %select_maximum_fusion = (f32[4096,256]{1,0:T(8,128)}, f32[4096,256]{1,0:T(8,128)}) fusion(f32[4096,32]{1,0:T(8,128)S(1)} %get-tuple-element.39, f32[4096,6]{1,0:T(8,128)S(1)} %copy-done.2, f32[4096,32]{1,0:T(8,128)S(1)} %get-tuple-element.40, f32[4096,6]{1,0:T(8,128)S(1)} %copy.25), kind=kLoop, calls=%fused_computation.8 | loop fusion | flops 8388608 | bytes 9633792 | tf_op jit(solution)/shard_map/concatenate | solution.py:388
  89.2 0.6 copy.29
  89.8 26.6 %shard_map.83 = (s32[8192]{0:T(1024)}, s32[2]{0:T(128)}) custom-call(s32[1]{0:T(128)} %bitcast.tile_ref, s32[8192]{0:T(1024)} %bitcast.56), custom_call_target="tpu_custom_call" | custom-call | flops 40000000 | bytes 20000000 | tf_op jit(solution)/shard_map/pallas_call | solution.py:64
  116.5 8.7 %shard_map.82.field_ref = f32[2048,384]{1,0:T(8,128)S(1)} custom-call(f32[32,64,384]{2,1,0:T(8,128)} %state_ref.1, f32[2,64,384]{2,1,0:T(8,128)S(1)} %collective-permute-done.west_ref, f32[2,64,384]{2,1,0:T(8,128)S(1)} %collective-permute-done.1.east_ref, f32[36,2,384]{2,1,0:T(2,128)S(1)} %collective-permute-done.2.south_ref, ...), custom_call_target="tpu_custom_call" | custom-call | tf_op jit(solution)/shard_map/pallas_call | solution.py:120
  125.2 6.6 %shard_map.84.x_ref = f32[32,16,128]{2,1,0:T(8,128)S(1)} custom-call(s32[2]{0:T(128)S(1)} %copy-done.1, s32[8192]{0:T(1024)S(1)} %copy-done, s32[8192]{0:T(1024)S(1)} %bitcast.45, f32[2048,384]{1,0:T(8,128)S(1)} %shard_map.82.field_ref, f32[4096,256]{1,0:T(8,128)} %get-tuple-element.42.table_ref), custom_call_target="tpu_custom_call" | custom-call | tf_op jit(solution)/shard_map/pallas_call | solution.py:210
  131.8 10.1 %shard_map.85.rest_0_.one_ref = f32[128,128]{1,0:T(8,128)S(1)} custom-call(f32[32,16,128]{2,1,0:T(8,128)S(1)} %shard_map.84.x_ref), custom_call_target="tpu_custom_call" | custom-call | tf_op jit(solution)/shard_map/pallas_call | solution.py:286
  141.9 6.8 %shard_map.86.x_ref = f32[32,16,128]{2,1,0:T(8,128)S(1)} custom-call(s32[2]{0:T(128)S(1)} %copy-done.1, s32[8192]{0:T(1024)S(1)} %copy-done, s32[8192]{0:T(1024)S(1)} %bitcast.46, f32[2048,384]{1,0:T(8,128)S(1)} %shard_map.82.field_ref, f32[4096,256]{1,0:T(8,128)} %get-tuple-element.41.table_ref, f32[128,128]{1,0:T(8,128)S(1)} %shard_map.85.rest_0_.one_ref), custom_call_target="tpu_custom_call" | custom-call | tf_op jit(solution)/shard_map/pallas_call | solution.py:210
  148.7 27.6 %shard_map.87.two_ref = f32[128,128]{1,0:T(8,128)S(1)} custom-call(f32[32,16,128]{2,1,0:T(8,128)S(1)} %shard_map.86.x_ref), custom_call_target="tpu_custom_call" | custom-call | tf_op jit(solution)/shard_map/pallas_call | solution.py:286
  176.3 4.0 %shard_map.88 = f32[2048,384]{1,0:T(8,128)} custom-call(f32[2048,384]{1,0:T(8,128)S(1)} %shard_map.82.field_ref, f32[128,128]{1,0:T(8,128)S(1)} %shard_map.85.rest_0_.one_ref, f32[128,128]{1,0:T(8,128)S(1)} %shard_map.87.two_ref), custom_call_target="tpu_custom_call" | custom-call | tf_op jit(solution)/shard_map/pallas_call | solution.py:313
  (31 shorter events, 0.6 us)
Async XLA Ops:
  1.1 82.2 %collective-permute-start = (f32[2,64,384]{2,1,0:T(8,128)S(1)}, f32[2,64,384]{2,1,0:T(8,128)S(1)}, u32[]{:S(2)}, u32[]{:S(2)}) collective-permute-start(f32[2,64,384]{2,1,0:T(8,128)S(1)} %get-tuple-element.12), channel_id=1, source_target_pairs={{0,2},{2,4},{4,6},{6,8},{8,10},{10,12},{12,14},{14,16},{16,18},{18... | collective-permute-start | bytes 589832 | tf_op jit(solution)/shard_map/ppermute | solution.py:331
  1.6 81.8 %collective-permute-start.1 = (f32[2,64,384]{2,1,0:T(8,128)S(1)}, f32[2,64,384]{2,1,0:T(8,128)S(1)}, u32[]{:S(2)}, u32[]{:S(2)}) collective-permute-start(f32[2,64,384]{2,1,0:T(8,128)S(1)} %get-tuple-element.11), channel_id=1, source_target_pairs={{2,0},{4,2},{6,4},{8,6},{10,8},{12,10},{14,12},{16,14},{18,16},{20... | collective-permute-start | bytes 589832 | tf_op jit(solution)/shard_map/ppermute | solution.py:331
  10.3 2.8 %copy-start.3 = (s32[2,4096]{1,0:T(2,128)S(1)}, s32[2,4096]{1,0:T(2,128)}, u32[]{:S(2)}) copy-start(s32[2,4096]{1,0:T(2,128)} %param.9) | copy-start | bytes 98308
  10.3 2.8 %copy-start.4 = (s32[2,4096]{1,0:T(2,128)S(1)}, s32[2,4096]{1,0:T(2,128)}, u32[]{:S(2)}) copy-start(s32[2,4096]{1,0:T(2,128)} %param.10) | copy-start | bytes 98308
  10.4 2.8 %copy-start.5 = (s32[1,1,2,16]{3,2,1,0:T(2,128)S(1)}, s32[1,1,2,16]{3,2,1,0:T(2,128)}, u32[]{:S(2)}) copy-start(s32[1,1,2,16]{3,2,1,0:T(2,128)} %param.15) | copy-start | bytes 388
  78.8 6.8 %copy-start.2 = (f32[4096,6]{1,0:T(8,128)S(1)}, f32[4096,6]{1,0:T(8,128)}, u32[]{:S(2)}) copy-start(f32[4096,6]{1,0:T(8,128)} %copy.27) | copy-start | bytes 294916
  83.4 33.1 %collective-permute-start.3 = (f32[36,2,384]{2,1,0:T(2,128)S(1)}, f32[36,2,384]{2,1,0:T(2,128)S(1)}, u32[]{:S(2)}, u32[]{:S(2)}) collective-permute-start(f32[36,2,384]{2,1,0:T(2,128)S(1)} %pad_maximum_fusion.1), channel_id=1, source_target_pairs={{1,0},{0,1},{3,2},{2,3},{5,4},{4,5},{7,6},{6,7},{9,8},{8,9},{11,10... | collective-permute-start | bytes 331784 | tf_op jit(solution)/shard_map/ppermute | solution.py:331
  83.9 32.6 %collective-permute-start.2 = (f32[36,2,384]{2,1,0:T(2,128)S(1)}, f32[36,2,384]{2,1,0:T(2,128)S(1)}, u32[]{:S(2)}, u32[]{:S(2)}) collective-permute-start(f32[36,2,384]{2,1,0:T(2,128)S(1)} %pad_maximum_fusion), channel_id=1, source_target_pairs={{0,1},{1,0},{2,3},{3,2},{4,5},{5,4},{6,7},{7,6},{8,9},{9,8},{10,11... | collective-permute-start | bytes 331784 | tf_op jit(solution)/shard_map/ppermute | solution.py:331
  116.4 8.8 %copy-start = (s32[8192]{0:T(1024)S(1)}, s32[8192]{0:T(1024)}, u32[]{:S(2)}) copy-start(s32[8192]{0:T(1024)} %get-tuple-element.8.order_ref) | copy-start | bytes 98308
  116.5 8.8 %copy-start.1 = (s32[2]{0:T(128)S(1)}, s32[2]{0:T(128)}, u32[]{:S(2)}) copy-start(s32[2]{0:T(128)} %get-tuple-element.7.count_ref) | copy-start | bytes 28

commit v2 on v1

--- a/solution.py
+++ b/solution.py
@@ -42,35 +42,92 @@
     return high, low
 
 
-def compact_kernel(nobs, tile_ref, owner_ref, order_ref, count_ref):
-    me = tile_ref[0]
-    step = 16
-    for batch in range(2):
-        base = batch * nobs
-
-        def body(i, count):
-            first = i * step
-            owners = [owner_ref[base + first + k] for k in range(step)]
-            for k in range(step):
-                order_ref[base + count] = first + k
-                count = count + jnp.where(owners[k] == me, 1, 0)
-            return count
-
-        count_ref[batch] = lax.fori_loop(0, nobs // step, body, 0)
-
-
-def compact(tile, owners):
-    batches, nobs = owners.shape
+def prepare_kernel(tiles_east, tiles_north, pattern_ref, owner_ref, all_ref, list_ref, ranks, held, send_sem, recv_sem):
+    tiles = tiles_east * tiles_north
+    me = lax.axis_index("gx") * tiles_north + lax.axis_index("gy")
+
+    def device(t):
+        return (t // tiles_north, lax.rem(t, tiles_north))
+
+    barrier = pltpu.get_barrier_semaphore()
+
+    def greet(d, carry):
+        pl.semaphore_signal(
+            barrier, inc=1, device_id=device(lax.rem(me + d, tiles)), device_id_type=pl.DeviceIdType.MESH
+        )
+        return carry
+
+    lax.fori_loop(1, tiles, greet, 0)
+    pl.semaphore_wait(barrier, tiles - 1)
+
+    def send(d, carry):
+        pltpu.make_async_remote_copy(
+            src_ref=pattern_ref,
+            dst_ref=held.at[d - 1],
+            send_sem=send_sem,
+            recv_sem=recv_sem,
+            device_id=device(lax.rem(me + d, tiles)),
+            device_id_type=pl.DeviceIdType.MESH,
+        ).start()
+        return carry
+
+    lax.fori_loop(1, tiles, send, 0)
+
+    rows = owner_ref.shape[0]
+    sub = lax.broadcasted_iota(jnp.int32, (LANES, LANES), 0)
+    lane = lax.broadcasted_iota(jnp.int32, (LANES, LANES), 1)
+    mine = jnp.where(owner_ref[...] == me, 1.0, 0.0)
+    before = jnp.where(sub < lane, 1.0, 0.0).astype(BF16)
+    ranks[...] = jnp.where(mine > 0.5, half_dot(mine.astype(BF16), before), -1.0)
+    place = lax.broadcasted_iota(jnp.int32, (16, LANES), 1).astype(F32).astype(BF16)
+    slot = sub.astype(F32)
+
+    def listed(i, carry):
+        block = ranks[pl.ds(pl.multiple_of(i * 8, 8), 8), :]
+        found = []
+        for k in range(8):
+            hot = jnp.where(block[k : k + 1] == slot, 1.0, 0.0).astype(BF16)
+            found.append(
+                lax.dot_general(place, hot, (((1,), (1,)), ((), ())), preferred_element_type=F32)[0:1]
+            )
+        rows8 = jnp.concatenate(found, axis=0)
+        number = jnp.sum(jnp.where(block >= 0.0, 1.0, 0.0), axis=1, keepdims=True)
+        list_ref[pl.ds(pl.multiple_of(i * 8, 8), 8), :] = (rows8 + 256.0 * number).astype(jnp.int32)
+        return carry
+
+    lax.fori_loop(0, rows // 8, listed, 0)
+    all_ref[me] = pattern_ref[...]
+    pltpu.make_async_copy(held, held, recv_sem).wait()
+    pltpu.make_async_copy(held, held, send_sem).wait()
+
+    def place_one(d, carry):
+        all_ref[lax.rem(me - d + tiles, tiles)] = held[d - 1]
+        return carry
+
+    lax.fori_loop(1, tiles, place_one, 0)
+
+
+def prepare(tiles_east, tiles_north, pattern, owners):
+    tiles = tiles_east * tiles_north
+    flat = pattern.reshape(1, -1).astype(F32)
+    flat = jnp.pad(flat, ((0, 0), (0, LANES - flat.shape[1])))
+    rows = owners.reshape(-1, LANES)
     return pl.pallas_call(
-        functools.partial(compact_kernel, nobs),
+        functools.partial(prepare_kernel, tiles_east, tiles_north),
         out_shape=(
-            jax.ShapeDtypeStruct((batches * nobs,), jnp.int32),
-            jax.ShapeDtypeStruct((batches,), jnp.int32),
+            jax.ShapeDtypeStruct((tiles, 1, LANES), F32),
+            jax.ShapeDtypeStruct(rows.shape, jnp.int32),
         ),
-        in_specs=[smem, smem],
-        out_specs=(smem, smem),
-        cost_estimate=pl.CostEstimate(flops=40_000_000, bytes_accessed=20_000_000, transcendentals=0),
-    )(tile, owners.reshape(-1))
+        in_specs=[vmem, vmem],
+        out_specs=(vmem, vmem),
+        scratch_shapes=[
+            pltpu.VMEM(rows.shape, F32),
+            pltpu.VMEM((tiles - 1, 1, LANES), F32),
+            pltpu.SemaphoreType.DMA,
+            pltpu.SemaphoreType.DMA,
+        ],
+        compiler_params=pltpu.CompilerParams(collective_id=1, has_side_effects=True),
+    )(flat, rows)
 
 
 def forecast_kernel(state_ref, west_ref, east_ref, south_ref, north_ref, out_ref, wide, middle):
@@ -130,51 +187,64 @@
     )(state, west, east, south, north)
 
 
-def sums_kernel(batch, nobs, tiles, mixed, count_ref, order_ref, cell_ref, field_ref, table_ref, *rest):
+def sums_kernel(batch, nobs, tiles, mixed, list_ref, cell_ref, field_ref, table_ref, *rest):
     if mixed:
         mix_ref, out_ref, picked, params, total = rest
     else:
         out_ref, picked, params, total = rest
-    count = count_ref[batch]
     base = batch * nobs
+    blocks = nobs // LANES
     total[...] = jnp.zeros_like(total)
     lane = lax.broadcasted_iota(jnp.int32, (CHUNK, LANES), 1)
     group = lane // ENS
     row = lax.broadcasted_iota(jnp.int32, (CHUNK, 1), 0)
-    width = table_ref.shape[1] - LANES
-    tile_of_row = lax.broadcasted_iota(jnp.int32, (width, 256), 0)
+    width = table_ref.shape[1]
+    first_lane = 16 + batch * tiles
+    tile_of_row = lax.broadcasted_iota(jnp.int32, (width, 256), 0) - first_lane
     tile_of_lane = lax.broadcasted_iota(jnp.int32, (width, 256), 1) // ENS
 
-    def chunk(ci, carry):
+    def block_of(c, start):
+        number = lax.shift_right_logical(list_ref[batch * blocks + c, 0], 8)
+
         def pick(i, carry):
-            for k in range(8):
-                at = i * 8 + k
-                place = ci * CHUNK + at
-                j = jnp.where(place < count, order_ref[base + place], 0)
+            for k in range(4):
+                j = c * LANES + (list_ref[batch * blocks + c, i * 4 + k] & 255)
+                at = start + i * 4 + k
                 picked[pl.ds(at, 1), :] = field_ref[pl.ds(cell_ref[base + j], 1), :]
                 params[pl.ds(at, 1), :] = table_ref[pl.ds(j, 1), :]
             return carry
 
-        lax.fori_loop(0, CHUNK // 8, pick, 0)
-        param = params[:, 0:LANES]
+        lax.fori_loop(0, lax.shift_right_logical(number + 3, 2), pick, 0)
+        return start + number
+
+    count = lax.fori_loop(0, blocks, block_of, 0)
+
+    def chunk(ci, carry):
+        rows = pl.ds(pl.multiple_of(ci * CHUNK, CHUNK), CHUNK)
+        valid = ci * CHUNK + row < count
+        param = jnp.where(valid, params[rows, 0:LANES], 0.0)
+        column = batch * 8
         values = (
-            param[:, 0:1] * picked[:, 0:LANES]
-            + param[:, 1:2] * picked[:, LANES : 2 * LANES]
-            + param[:, 2:3] * picked[:, 2 * LANES : 3 * LANES]
+            param[:, column : column + 1] * picked[rows, 0:LANES]
+            + param[:, column + 1 : column + 2] * picked[rows, LANES : 2 * LANES]
+            + param[:, column + 2 : column + 3] * picked[rows, 2 * LANES : 3 * LANES]
         )
-        values = jnp.where(group.astype(F32) == param[:, 3:4], values, 0.0)
+        values = jnp.where(valid & (group.astype(F32) == param[:, column + 3 : column + 4]), values, 0.0)
         values = values + pltpu.roll(values, 64, 1)
         values = values + pltpu.roll(values, 32, 1)
         if mixed:
             values = exact_dot(values, mix_ref[...])
         centre = jnp.sum(values, axis=1, keepdims=True) / float(LANES)
-        inverse_error = param[:, 5:6]
+        inverse_error = param[:, column + 5 : column + 6]
         deviation = (values - centre) * inverse_error
-        innovation = (param[:, 4:5] - centre) * inverse_error
-        rho = jnp.where(ci * CHUNK + row < count, params[:, LANES:], 0.0)
+        innovation = (param[:, column + 4 : column + 5] - centre) * inverse_error
         left = jnp.where(group == 0, deviation, jnp.where(lane == ENS, innovation, 0.0))
         high, low = split(left.T[0:48])
         both = jnp.concatenate([high, low], axis=0)
+        if width == LANES:
+            rho = param
+        else:
+            rho = jnp.where(valid, params[rows, :], 0.0)
         rho_high, rho_low = split(rho)
         pair = jnp.concatenate([deviation, deviation], axis=1)
         for g in range(tiles // 8):
@@ -199,26 +269,26 @@
                 packed = jnp.where(small == r, moved, packed)
             proj = pltpu.roll(blocks[4], (-32 * t) % LANES, 1) if t else blocks[4]
             out_ref[q * 4 + t, 0:8, :] = packed
-            out_ref[q * 4 + t, 8:16, :] = jnp.where(small == 0, proj, 0.0)
+            out_ref[q * 4 + t, 8:9, :] = jnp.where(small == 0, proj, 0.0)[0:1]
         return carry
 
     lax.fori_loop(0, tiles // 4, pack, 0)
 
 
-def own_sums(batch, nobs, tiles, counts, order, cells, field, table, mix=None):
+def own_sums(batch, nobs, tiles, lists, cells, field, table, mix=None):
     extra = [] if mix is None else [mix]
     return pl.pallas_call(
         functools.partial(sums_kernel, batch, nobs, tiles, mix is not None),
-        out_shape=jax.ShapeDtypeStruct((tiles, 16, LANES), F32),
-        in_specs=[smem] * 3 + [vmem] * (2 + len(extra)),
+        out_shape=jax.ShapeDtypeStruct((tiles, 9, LANES), F32),
+        in_specs=[smem] * 2 + [vmem] * (2 + len(extra)),
         out_specs=vmem,
         scratch_shapes=[
-            pltpu.VMEM((CHUNK, COMP * LANES), F32),
-            pltpu.VMEM((CHUNK, table.shape[1]), F32),
+            pltpu.VMEM((nobs + 8, COMP * LANES), F32),
+            pltpu.VMEM((nobs + 8, table.shape[1]), F32),
             pltpu.VMEM((48, tiles * ENS), F32),
         ],
         compiler_params=pltpu.CompilerParams(vmem_limit_bytes=VMEM_LIMIT),
-    )(counts, order, cells, field, table, *extra)
+    )(lists, cells, field, table, *extra)
 
 
 def mix_kernel(tiles_east, tiles_north, x_ref, out_ref, held, send_sem, recv_sem):
@@ -265,9 +335,13 @@
     system = (ENS - 1.0) * unit + cov
     bound = jnp.max(jnp.sum(jnp.abs(system), axis=1, keepdims=True), axis=0, keepdims=True)
     approach, root = system / bound, unit
-    for sweep in range(NSIT):
+    middle = 1.5 * unit - 0.5 * approach
+    approach, root = exact_dot(approach, middle), middle
+    for sweep in range(1, NSIT):
         middle = 1.5 * unit - 0.5 * exact_dot(root, approach)
-        approach, root = exact_dot(approach, middle), exact_dot(middle, root)
+        if sweep < NSIT - 1:
+            approach = exact_dot(approach, middle)
+        root = exact_dot(middle, root)
     inverse = exact_dot(root, root) / bound
     weights = jnp.sum(inverse * proj, axis=1, keepdims=True)
     shifts = weights + math.sqrt(ENS - 1.0) * root / jnp.sqrt(bound)
@@ -289,7 +363,7 @@
         in_specs=[vmem],
         out_specs=vmem,
         scratch_shapes=[
-            pltpu.VMEM((tiles - 1, 16, LANES), F32),
+            pltpu.VMEM((tiles - 1, 9, LANES), F32),
             pltpu.SemaphoreType.DMA,
             pltpu.SemaphoreType.DMA,
         ],
@@ -354,7 +428,6 @@
     tiles_east = lax.axis_size("gx")
     tiles_north = lax.axis_size("gy")
     tiles = tiles_east * tiles_north
-    own_tile = lax.axis_index("gx") * tiles_north + lax.axis_index("gy")
     nobs = obs_owner.shape[1]
 
     west, east = neighbours("gx", state[-2:], state[:2])
@@ -362,42 +435,32 @@
     initial = jnp.concatenate([west[:, :2], state[:, :2], east[:, :2]], axis=0)
     south, north = neighbours("gy", last, initial)
 
-    patterns = lax.all_gather(pattern[0, 0], ("gx", "gy"))
-    order, counts = compact(jnp.reshape(own_tile, (1,)).astype(jnp.int32), obs_owner)
+    patterns, lists = prepare(tiles_east, tiles_north, pattern[0, 0], obs_owner)
     cells = obs_cell.reshape(-1)
-    width = -(-tiles // LANES) * LANES
-    tables = []
+    blocks = pattern.shape[3]
+    patterns = patterns[:, 0, : 2 * blocks].reshape(tiles, 2, blocks)
+    width = -(-(16 + 2 * tiles) // LANES) * LANES
+    columns, rhos = [], []
     for batch in range(2):
-        blocks = patterns.shape[2]
         rho = distance_weights(
             obs_owner[batch], obs_cell[batch], span_east, span_north, tiles_east, tiles_north
         ).reshape(blocks, nobs // blocks, tiles)
-        rho = (rho * patterns[:, batch].T.astype(F32)[:, None, :]).reshape(nobs, tiles)
-        columns = jnp.stack(
-            [
-                obs_coef[batch, 0],
-                obs_coef[batch, 1],
-                obs_coef[batch, 2],
-                obs_level[batch].astype(F32),
-                obs_value[batch],
-                1.0 / obs_error[batch],
-            ],
-            axis=1,
-        )
-        tables.append(
-            jnp.concatenate(
-                [
-                    jnp.pad(columns, ((0, 0), (0, LANES - columns.shape[1]))),
-                    jnp.pad(rho, ((0, 0), (0, width - tiles))),
-                ],
-                axis=1,
-            )
-        )
+        rhos.append((rho * patterns[:, batch].T[:, None, :]).reshape(nobs, tiles))
+        columns += [
+            obs_coef[batch],
+            obs_level[batch][None].astype(F32),
+            obs_value[batch][None],
+            1.0 / obs_error[batch][None],
+            jnp.zeros((2, nobs), F32),
+        ]
+    columns = jnp.concatenate(columns, axis=0).T
+    spare = jnp.zeros((nobs, width - 16 - 2 * tiles), F32)
+    table = jnp.concatenate([columns, *rhos, spare], axis=1)
 
     field = forecast(state, west, east, south, north)
-    sums = own_sums(0, nobs, tiles, counts, order, cells, field, tables[0])
+    sums = own_sums(0, nobs, tiles, lists, cells, field, table)
     first_mix = tile_mix(tiles_east, tiles_north, sums)
-    sums = own_sums(1, nobs, tiles, counts, order, cells, field, tables[1], first_mix)
+    sums = own_sums(1, nobs, tiles, lists, cells, field, table, first_mix)
     second_mix = tile_mix(tiles_east, tiles_north, sums)
     return apply_mix(field, first_mix, second_mix).reshape(span_east, span_north, features)
 

time: 182 us -> 107 us (0.59)
  blocking collectives: 65.3 us -> 0 us
  Pallas kernels: 90.4 us -> 77.3 us
  waiting for transfers between devices: 0.01 us -> 3.84 us
    all_gather x1 -> x0, blocking collectives: 65.3 us -> none  [local(): patterns = lax.all_gather(pattern[0, 0], ('gx', 'gy'))]
    pallas_call x1, Pallas kernels: 26.6 us -> 9.38 us  [prepare(): pl.pallas_call(functools.partial(prepare_kernel, tiles_east, tiles_north)...]
    pallas_call x2, Pallas kernels: 37.7 us -> 43.5 us  [tile_mix(): pl.pallas_call(functools.partial(mix_kernel, tiles_east, tiles_north), ou...]
    another operation x6 -> x1, local copies, waits for them, and re-layouts: 4.71 us -> 0.01 us  [local(): jnp.stack([obs_coef[batch, 0], obs_coef[batch, 1], obs_coef[batch, 2], ob...]
    ppermute x4, waiting for transfers between devices: 0.01 us -> 3.84 us  [neighbours(): return (lax.ppermute(last, axis, up), lax.ppermute(initial, axis, down))]
    concatenate x1, other arithmetic: 3.57 us -> 1.15 us  [local(): table = jnp.concatenate([columns, *rhos, spare], axis=1)]
    slice x0 -> x2, local copies, waits for them, and re-layouts: none -> 1.85 us  [the longest x1 1.06 us: local(): obs_coef[batch]]
  transfers between devices with their start and end apart: 4 -> 4, of which waited for: 0 -> 2; matrix products, arithmetic and copies ran while one was open for 9% -> 14% of each run, Pallas kernels for 15% -> 9%
where the time goes in v2:
time: 107 us; the launch traced here: 105 us
  Pallas kernels  77.3 us (72%)
  local copies, waits for them, and re-layouts  8.92 us (8%)
  starting transfers between devices  7.69 us (7%)
  other arithmetic  7.07 us (7%)
  waiting for transfers between devices  3.84 us (4%)
    pallas_call x2, Pallas kernels, tile_mix(): pl.pallas_call(functools.partial(mix_kernel, tiles_east, tiles_north), ou...  43.5 us
    pallas_call x2, Pallas kernels, own_sums(): pl.pallas_call(functools.partial(sums_kernel, batch, nobs, tiles, mix is...  11.7 us
    pallas_call x1, Pallas kernels, prepare(): pl.pallas_call(functools.partial(prepare_kernel, tiles_east, tiles_north)...  9.38 us
    pallas_call x1, Pallas kernels, forecast(): pl.pallas_call(forecast_kernel, out_shape=jax.ShapeDtypeStruct((nx * ny,...  8.72 us
    ppermute x4, starting transfers between devices, neighbours(): return (lax.ppermute(last, axis, up), lax.ppermute(initial, axis, down))  7.69 us
    pallas_call x1, Pallas kernels, apply_mix(): pl.pallas_call(apply_kernel, out_shape=jax.ShapeDtypeStruct((rows, feat),...  3.99 us
    ppermute x4, waiting for transfers between devices, neighbours(): return (lax.ppermute(last, axis, up), lax.ppermute(initial, axis, down))  3.84 us
    mul x1, other arithmetic, local(): rhos.append((rho * patterns[:, batch].T[:, None, :]).reshape(nobs, tiles))  3.3 us
  transfers between devices with their start and end apart: 4, of which 2 were waited for; matrix products, arithmetic and copies ran while one was open for 14% of the time, Pallas kernels for 9%

profile of v2, /device:TPU:0, one launch (start us, length us, event | category | flops | bytes accessed | tf_op | source)
XLA Modules:
  0.0 105.0 jit_solution(1292263743657517190)
XLA Ops:
  0.0 1.0 fusion.43
  1.6 5.0 %collective-permute-start.1 = (f32[2,64,384]{2,1,0:T(8,128)S(1)}, f32[2,64,384]{2,1,0:T(8,128)S(1)}, u32[]{:S(2)}, u32[]{:S(2)}) collective-permute-start(f32[2,64,384]{2,1,0:T(8,128)S(1)} %get-tuple-element.11), channel_id=1, source_target_pairs={{2,0},{4,2},{6,4},{8,6},{10,8},{12,10},{14,12},{16,14},{18,16},{20... | collective-permute-start | bytes 589832 | tf_op jit(solution)/shard_map/ppermute | solution.py:405
  6.6 0.9 fusion.49
  7.5 1.4 %reshape.350.owner_ref = s32[64,128]{1,0:T(8,128)} reshape(s32[2,4096]{1,0:T(2,128)} %param.9) | data formatting | bytes 65536 | tf_op jit(solution)/shard_map/reshape | solution.py:114
  8.9 0.9 fusion.48
  9.7 0.7 convert_element_type.72
  11.1 9.4 %shard_map.83 = (f32[32,1,128]{2,1,0:T(1,128)}, s32[64,128]{1,0:T(8,128)}) custom-call(f32[1,128]{1,0:T(1,128)} %pad.4.pattern_ref, s32[64,128]{1,0:T(8,128)} %reshape.350.owner_ref), custom_call_target="tpu_custom_call" | custom-call | tf_op jit(solution)/shard_map/pallas_call | solution.py:115
  20.5 0.8 copy.40
  21.3 1.1 %fusion.46 = (f32[1,3,4096]{2,0,1:T(1,128)S(1)}, f32[1,3,4096]{2,0,1:T(1,128)S(1)}) fusion(f32[2,3,4096]{2,0,1:T(2,128)} %param.12), kind=kLoop, calls=%fused_computation.94 | loop fusion | bytes 196608 | tf_op jit(solution)/shard_map/slice | solution.py:450
  22.3 0.9 slice_convert_fusion
  23.3 0.9 slice_divide_fusion
  25.2 3.3 %fusion.5 = (f32[4096,32]{1,0:T(8,128)S(1)}, f32[4096,32]{1,0:T(8,128)S(1)}) fusion(f32[16,32]{1,0:T(8,128)S(1)} %get-tuple-element.33, f32[32]{0:T(128)S(1)} %get-tuple-element.39, f32[4096]{0:T(1024)S(1)} %get-tuple-element.26, f32[32]{0:T(128)S(1)} %get-tuple-element.40, f32[4096]{0:T(1024)S(1)} %get-tuple-element.25, f32[16,32]{1,0:T(8,128)S(1)} %get-tuple-element.34, ...), kind=kLoop, calls=%fused_computation.13 | loop fusion | flops 5505024 | bytes 1118464 | tf_op jit(solution)/shard_map/mul | solution.py:448
  28.5 1.2 %fusion.42 = (f32[32,2,384]{2,1,0:T(2,128)S(1)}, f32[32,2,384]{2,1,0:T(2,128)S(1)}) fusion(f32[32,64,384]{2,1,0:T(8,128)} %state_ref.1), kind=kLoop, calls=%fused_computation.90 | loop fusion | bytes 393216 | tf_op jit(solution)/shard_map/slice | solution.py:435
  29.8 1.5 %collective-permute-start.3 = (f32[36,2,384]{2,1,0:T(2,128)S(1)}, f32[36,2,384]{2,1,0:T(2,128)S(1)}, u32[]{:S(2)}, u32[]{:S(2)}) collective-permute-start(f32[36,2,384]{2,1,0:T(2,128)S(1)} %pad_maximum_fusion.1), channel_id=1, source_target_pairs={{1,0},{0,1},{3,2},{2,3},{5,4},{4,5},{7,6},{6,7},{9,8},{8,9},{11,10... | collective-permute-start | bytes 331784 | tf_op jit(solution)/shard_map/ppermute | solution.py:405
  31.4 0.6 collective-permute-start.2
  32.0 1.1 %maximum_maximum_fusion.table_ref = f32[4096,128]{1,0:T(8,128)S(1)} fusion(f32[4096,32]{1,0:T(8,128)S(1)} %get-tuple-element.36, f32[4096,32]{1,0:T(8,128)S(1)} %get-tuple-element.35, f32[4096,16]{1,0:T(8,128)S(1)} %bitcast.28, f32[128]{0:T(128)S(1)} %pad.8.clone), kind=kLoop, calls=%fused_computation.24 | loop fusion | flops 1572864 | bytes 3408384 | tf_op jit(solution)/shard_map/concatenate | solution.py:458
  33.2 2.5 %collective-permute-done.3.north_ref = f32[36,2,384]{2,1,0:T(2,128)S(1)} collective-permute-done((f32[36,2,384]{2,1,0:T(2,128)S(1)}, f32[36,2,384]{2,1,0:T(2,128)S(1)}, u32[]{:S(2)}, u32[]{:S(2)}) %collective-permute-start.3) | collective-permute-done | bytes 110624 | tf_op jit(solution)/shard_map/ppermute | solution.py:405
  35.8 1.3 %collective-permute-done.2.south_ref = f32[36,2,384]{2,1,0:T(2,128)S(1)} collective-permute-done((f32[36,2,384]{2,1,0:T(2,128)S(1)}, f32[36,2,384]{2,1,0:T(2,128)S(1)}, u32[]{:S(2)}, u32[]{:S(2)}) %collective-permute-start.2) | collective-permute-done | bytes 110624 | tf_op jit(solution)/shard_map/ppermute | solution.py:405
  37.1 8.7 %shard_map.82.field_ref = f32[2048,384]{1,0:T(8,128)S(1)} custom-call(f32[32,64,384]{2,1,0:T(8,128)} %state_ref.1, f32[2,64,384]{2,1,0:T(8,128)S(1)} %collective-permute-done.west_ref, f32[2,64,384]{2,1,0:T(8,128)S(1)} %collective-permute-done.1.east_ref, f32[36,2,384]{2,1,0:T(2,128)S(1)} %collective-permute-done.2.south_ref, ...), custom_call_target="tpu_custom_call" | custom-call | tf_op jit(solution)/shard_map/pallas_call | solution.py:177
  45.8 5.6 %shard_map.84.x_ref = f32[32,9,128]{2,1,0:T(8,128)S(1)} custom-call(s32[64,128]{1,0:T(8,128)S(1)} %copy-done, s32[8192]{0:T(1024)S(1)} %bitcast.26, f32[2048,384]{1,0:T(8,128)S(1)} %shard_map.82.field_ref, f32[4096,128]{1,0:T(8,128)S(1)} %maximum_maximum_fusion.table_ref), custom_call_target="tpu_custom_call" | custom-call | tf_op jit(solution)/shard_map/pallas_call | solution.py:280
  51.4 20.4 %shard_map.85.rest_0_.one_ref = f32[128,128]{1,0:T(8,128)S(1)} custom-call(f32[32,9,128]{2,1,0:T(8,128)S(1)} %shard_map.84.x_ref), custom_call_target="tpu_custom_call" | custom-call | tf_op jit(solution)/shard_map/pallas_call | solution.py:360
  71.8 6.1 %shard_map.86.x_ref = f32[32,9,128]{2,1,0:T(8,128)S(1)} custom-call(s32[64,128]{1,0:T(8,128)S(1)} %copy-done, s32[8192]{0:T(1024)S(1)} %bitcast.27, f32[2048,384]{1,0:T(8,128)S(1)} %shard_map.82.field_ref, f32[4096,128]{1,0:T(8,128)S(1)} %maximum_maximum_fusion.table_ref, f32[128,128]{1,0:T(8,128)S(1)} %shard_map.85.rest_0_.one_ref), custom_call_target="tpu_custom_call" | custom-call | tf_op jit(solution)/shard_map/pallas_call | solution.py:280
  77.9 23.1 %shard_map.87.two_ref = f32[128,128]{1,0:T(8,128)S(1)} custom-call(f32[32,9,128]{2,1,0:T(8,128)S(1)} %shard_map.86.x_ref), custom_call_target="tpu_custom_call" | custom-call | tf_op jit(solution)/shard_map/pallas_call | solution.py:360
  101.1 4.0 %shard_map.88 = f32[2048,384]{1,0:T(8,128)} custom-call(f32[2048,384]{1,0:T(8,128)S(1)} %shard_map.82.field_ref, f32[128,128]{1,0:T(8,128)S(1)} %shard_map.85.rest_0_.one_ref, f32[128,128]{1,0:T(8,128)S(1)} %shard_map.87.two_ref), custom_call_target="tpu_custom_call" | custom-call | tf_op jit(solution)/shard_map/pallas_call | solution.py:387
  (23 shorter events, 2.4 us)
Async XLA Ops:
  1.1 28.7 %collective-permute-start = (f32[2,64,384]{2,1,0:T(8,128)S(1)}, f32[2,64,384]{2,1,0:T(8,128)S(1)}, u32[]{:S(2)}, u32[]{:S(2)}) collective-permute-start(f32[2,64,384]{2,1,0:T(8,128)S(1)} %get-tuple-element.12), channel_id=1, source_target_pairs={{0,2},{2,4},{4,6},{6,8},{8,10},{10,12},{12,14},{14,16},{16,18},{18... | collective-permute-start | bytes 589832 | tf_op jit(solution)/shard_map/ppermute | solution.py:405
  1.6 28.2 %collective-permute-start.1 = (f32[2,64,384]{2,1,0:T(8,128)S(1)}, f32[2,64,384]{2,1,0:T(8,128)S(1)}, u32[]{:S(2)}, u32[]{:S(2)}) collective-permute-start(f32[2,64,384]{2,1,0:T(8,128)S(1)} %get-tuple-element.11), channel_id=1, source_target_pairs={{2,0},{4,2},{6,4},{8,6},{10,8},{12,10},{14,12},{16,14},{18,16},{20... | collective-permute-start | bytes 589832 | tf_op jit(solution)/shard_map/ppermute | solution.py:405
  29.8 5.9 %collective-permute-start.3 = (f32[36,2,384]{2,1,0:T(2,128)S(1)}, f32[36,2,384]{2,1,0:T(2,128)S(1)}, u32[]{:S(2)}, u32[]{:S(2)}) collective-permute-start(f32[36,2,384]{2,1,0:T(2,128)S(1)} %pad_maximum_fusion.1), channel_id=1, source_target_pairs={{1,0},{0,1},{3,2},{2,3},{5,4},{4,5},{7,6},{6,7},{9,8},{8,9},{11,10... | collective-permute-start | bytes 331784 | tf_op jit(solution)/shard_map/ppermute | solution.py:405
  31.4 5.7 %collective-permute-start.2 = (f32[36,2,384]{2,1,0:T(2,128)S(1)}, f32[36,2,384]{2,1,0:T(2,128)S(1)}, u32[]{:S(2)}, u32[]{:S(2)}) collective-permute-start(f32[36,2,384]{2,1,0:T(2,128)S(1)} %pad_maximum_fusion), channel_id=1, source_target_pairs={{0,1},{1,0},{2,3},{3,2},{4,5},{5,4},{6,7},{7,6},{8,9},{9,8},{10,11... | collective-permute-start | bytes 331784 | tf_op jit(solution)/shard_map/ppermute | solution.py:405
  32.0 1.2 %copy-start.1 = (s32[2,4096]{1,0:T(2,128)S(1)}, s32[2,4096]{1,0:T(2,128)}, u32[]{:S(2)}) copy-start(s32[2,4096]{1,0:T(2,128)} %param.10) | copy-start | bytes 98308
  33.2 12.6 %copy-start = (s32[64,128]{1,0:T(8,128)S(1)}, s32[64,128]{1,0:T(8,128)}, u32[]{:S(2)}) copy-start(s32[64,128]{1,0:T(8,128)} %get-tuple-element.7.list_ref) | copy-start | bytes 98308

commit v3 on v2

--- a/solution.py
+++ b/solution.py
@@ -207,14 +207,15 @@
         number = lax.shift_right_logical(list_ref[batch * blocks + c, 0], 8)
 
         def pick(i, carry):
-            for k in range(4):
-                j = c * LANES + (list_ref[batch * blocks + c, i * 4 + k] & 255)
-                at = start + i * 4 + k
-                picked[pl.ds(at, 1), :] = field_ref[pl.ds(cell_ref[base + j], 1), :]
-                params[pl.ds(at, 1), :] = table_ref[pl.ds(j, 1), :]
+            js = [c * LANES + (list_ref[batch * blocks + c, i * 8 + k] & 255) for k in range(8)]
+            values = [field_ref[pl.ds(cell_ref[base + j], 1), :] for j in js]
+            entries = [table_ref[pl.ds(j, 1), :] for j in js]
+            for k in range(8):
+                picked[pl.ds(start + i * 8 + k, 1), :] = values[k]
+                params[pl.ds(start + i * 8 + k, 1), :] = entries[k]
             return carry
 
-        lax.fori_loop(0, lax.shift_right_logical(number + 3, 2), pick, 0)
+        lax.fori_loop(0, lax.shift_right_logical(number + 7, 3), pick, 0)
         return start + number
 
     count = lax.fori_loop(0, blocks, block_of, 0)
@@ -245,11 +246,11 @@
             rho = param
         else:
             rho = jnp.where(valid, params[rows, :], 0.0)
-        rho_high, rho_low = split(rho)
+        rho_both = jnp.concatenate(split(rho), axis=1)
         pair = jnp.concatenate([deviation, deviation], axis=1)
         for g in range(tiles // 8):
             spread = jnp.where(tile_of_row == tile_of_lane + g * 8, 1.0, 0.0).astype(BF16)
-            weight = half_dot(rho_high, spread) + half_dot(rho_low, spread)
+            weight = half_dot(rho_both, jnp.concatenate([spread, spread], axis=0))
             right_high, right_low = split(weight * pair)
             first = half_dot(both, right_high)
             second = half_dot(high, right_low)
@@ -405,22 +406,69 @@
     return lax.ppermute(last, axis, up), lax.ppermute(initial, axis, down)
 
 
-def distance_weights(owners, cells, span_east, span_north, tiles_east, tiles_north):
-    grid_east, grid_north = span_east * tiles_east, span_north * tiles_north
-    place_east = (owners // tiles_north * span_east + cells // span_north).astype(F32)[:, None]
-    place_north = (owners % tiles_north * span_north + cells % span_north).astype(F32)[:, None]
-    tile = jnp.arange(tiles_east * tiles_north, dtype=jnp.int32)[None, :]
-    centre_east = (tile // tiles_north * span_east).astype(F32) + (span_east - 1) / 2.0
-    centre_north = (tile % tiles_north * span_north).astype(F32) + (span_north - 1) / 2.0
-    gap_east = place_east - centre_east
-    gap_east = jnp.where(gap_east >= grid_east / 2.0, gap_east - grid_east, gap_east)
-    gap_east = jnp.where(gap_east < -grid_east / 2.0, gap_east + grid_east, gap_east)
-    gap_north = place_north - centre_north
-    gap_north = jnp.where(gap_north >= grid_north / 2.0, gap_north - grid_north, gap_north)
-    gap_north = jnp.where(gap_north < -grid_north / 2.0, gap_north + grid_north, gap_north)
-    scale_east = gap_east / (radius_share * grid_east)
-    scale_north = gap_north / (radius_share * grid_north)
-    return jnp.exp(-0.5 * (scale_east * scale_east + scale_north * scale_north))
+def table_kernel(
+    nx, ny, tiles_east, tiles_north, blocks,
+    owner_ref, cell_ref, level_ref, coef_ref, value_ref, error_ref, pattern_ref, out_ref,
+):
+    tiles = tiles_east * tiles_north
+    nobs = owner_ref.shape[1]
+    width = out_ref.shape[1]
+    grid_east, grid_north = float(nx * tiles_east), float(ny * tiles_north)
+
+    def parts(value, size):
+        whole = jnp.floor((value + 0.5) * (1.0 / size))
+        return whole, value - whole * size
+
+    tile = lax.broadcasted_iota(jnp.int32, (tiles, LANES), 0).astype(F32)
+    tile_east, tile_north = parts(tile, tiles_north)
+    centre_east = tile_east * nx + (nx - 1) / 2.0
+    centre_north = tile_north * ny + (ny - 1) / 2.0
+    lane = lax.broadcasted_iota(jnp.int32, (tiles, LANES), 1)
+
+    def scaled(place, centre, grid):
+        gap = place - centre
+        gap = jnp.where(gap >= grid / 2.0, gap - grid, gap)
+        gap = jnp.where(gap < -grid / 2.0, gap + grid, gap)
+        return gap * (1.0 / (radius_share * grid))
+
+    def one(c, carry):
+        at = pl.ds(pl.multiple_of(c * LANES, LANES), LANES)
+        columns, rhos = [], []
+        for batch in range(2):
+            row = slice(batch, batch + 1)
+            owner_east, owner_north = parts(owner_ref[row, at].astype(F32), tiles_north)
+            cell_east, cell_north = parts(cell_ref[row, at].astype(F32), ny)
+            far_east = scaled(owner_east * nx + cell_east, centre_east, grid_east)
+            far_north = scaled(owner_north * ny + cell_north, centre_north, grid_north)
+            used = batch * blocks + (c * LANES) // (nobs // blocks)
+            mask = jnp.sum(jnp.where(lane == used, pattern_ref[...], 0.0), axis=1, keepdims=True)
+            rhos.append(mask * jnp.exp(-0.5 * (far_east * far_east + far_north * far_north)))
+            columns += [
+                coef_ref[3 * batch : 3 * batch + 3, at],
+                level_ref[row, at].astype(F32),
+                value_ref[row, at],
+                1.0 / error_ref[row, at],
+                jnp.zeros((2, LANES), F32),
+            ]
+        spare = jnp.zeros((width - 16 - 2 * tiles, LANES), F32)
+        out_ref[at, :] = jnp.concatenate([*columns, *rhos, spare], axis=0).T
+        return carry
+
+    lax.fori_loop(0, nobs // LANES, one, 0)
+
+
+def make_table(nx, ny, tiles_east, tiles_north, blocks, patterns, owner, cell, level, coef, value, error):
+    tiles = tiles_east * tiles_north
+    nobs = owner.shape[1]
+    width = -(-(16 + 2 * tiles) // LANES) * LANES
+    return pl.pallas_call(
+        functools.partial(table_kernel, nx, ny, tiles_east, tiles_north, blocks),
+        out_shape=jax.ShapeDtypeStruct((nobs, width), F32),
+        in_specs=[vmem] * 7,
+        out_specs=vmem,
+        compiler_params=pltpu.CompilerParams(vmem_limit_bytes=VMEM_LIMIT),
+        cost_estimate=pl.CostEstimate(flops=50_000_000, bytes_accessed=12_000_000, transcendentals=0),
+    )(owner, cell, level, coef.reshape(6, nobs), value, error, patterns.reshape(tiles, LANES))
 
 
 def local(state, obs_owner, obs_cell, obs_level, obs_coef, obs_value, obs_error, pattern):
@@ -431,31 +479,16 @@
     nobs = obs_owner.shape[1]
 
     west, east = neighbours("gx", state[-2:], state[:2])
+    patterns, lists = prepare(tiles_east, tiles_north, pattern[0, 0], obs_owner)
     last = jnp.concatenate([west[:, -2:], state[:, -2:], east[:, -2:]], axis=0)
     initial = jnp.concatenate([west[:, :2], state[:, :2], east[:, :2]], axis=0)
+    last, initial, patterns = lax.optimization_barrier((last, initial, patterns))
     south, north = neighbours("gy", last, initial)
-
-    patterns, lists = prepare(tiles_east, tiles_north, pattern[0, 0], obs_owner)
     cells = obs_cell.reshape(-1)
-    blocks = pattern.shape[3]
-    patterns = patterns[:, 0, : 2 * blocks].reshape(tiles, 2, blocks)
-    width = -(-(16 + 2 * tiles) // LANES) * LANES
-    columns, rhos = [], []
-    for batch in range(2):
-        rho = distance_weights(
-            obs_owner[batch], obs_cell[batch], span_east, span_north, tiles_east, tiles_north
-        ).reshape(blocks, nobs // blocks, tiles)
-        rhos.append((rho * patterns[:, batch].T[:, None, :]).reshape(nobs, tiles))
-        columns += [
-            obs_coef[batch],
-            obs_level[batch][None].astype(F32),
-            obs_value[batch][None],
-            1.0 / obs_error[batch][None],
-            jnp.zeros((2, nobs), F32),
-        ]
-    columns = jnp.concatenate(columns, axis=0).T
-    spare = jnp.zeros((nobs, width - 16 - 2 * tiles), F32)
-    table = jnp.concatenate([columns, *rhos, spare], axis=1)
+    table = make_table(
+        span_east, span_north, tiles_east, tiles_north, pattern.shape[3], patterns,
+        obs_owner, obs_cell, obs_level, obs_coef, obs_value, obs_error,
+    )
 
     field = forecast(state, west, east, south, north)
     sums = own_sums(0, nobs, tiles, lists, cells, field, table)

time: 107 us -> 99.2 us (0.927); the launches traced: 105 us -> 99.5 us
  other arithmetic: 7.07 us -> 0.8 us
  waiting for transfers between devices: 3.84 us -> 0.01 us
  Pallas kernels: 77.3 us -> 80.4 us
  local copies, waits for them, and re-layouts: 8.92 us -> 10.6 us
    unnamed x5 -> x16, local copies, waits for them, and re-layouts: 0.01 us -> 6.23 us
    pallas_call x0 -> x1, Pallas kernels: none -> 5.61 us  [make_table(): pl.pallas_call(functools.partial(table_kernel, nx, ny, tiles_east, tiles_...]
    ppermute x4, waiting for transfers between devices: 3.84 us -> 0.01 us  [neighbours(): return (lax.ppermute(last, axis, up), lax.ppermute(initial, axis, down))]
    slice x4 -> x0, local copies, waits for them, and re-layouts: 3.57 us -> none  [the longest x1 1.06 us: local(): obs_coef[batch]]
    mul x1 -> x0, other arithmetic: 3.3 us -> none  [local(): rhos.append((rho * patterns[:, batch].T[:, None, :]).reshape(nobs, tiles))]
    pallas_call x2, Pallas kernels: 43.5 us -> 40.4 us  [tile_mix(): pl.pallas_call(functools.partial(mix_kernel, tiles_east, tiles_north), ou...]
    concatenate x2 -> x0, other arithmetic: 1.2 us -> none  [the longest x1 1.15 us: local(): table = jnp.concatenate([columns, *rhos, spare], axis=1)]
  transfers between devices with their start and end apart: 4 -> 4, of which waited for: 2 -> 0; matrix products, arithmetic and copies ran while one was open for 14% -> 6% of each run, Pallas kernels for 9% -> 15%
where the time goes in v3:
time: 99.2 us; the launch traced here: 99.5 us
  Pallas kernels  80.4 us (81%)
  local copies, waits for them, and re-layouts  10.6 us (11%)
  starting transfers between devices  7.56 us (8%)
    pallas_call x2, Pallas kernels, tile_mix(): pl.pallas_call(functools.partial(mix_kernel, tiles_east, tiles_north), ou...  40.4 us
    pallas_call x2, Pallas kernels, own_sums(): pl.pallas_call(functools.partial(sums_kernel, batch, nobs, tiles, mix is...  12.3 us
    pallas_call x1, Pallas kernels, prepare(): pl.pallas_call(functools.partial(prepare_kernel, tiles_east, tiles_north)...  9.39 us
    pallas_call x1, Pallas kernels, forecast(): pl.pallas_call(forecast_kernel, out_shape=jax.ShapeDtypeStruct((nx * ny,...  8.72 us
    ppermute x4, starting transfers between devices, neighbours(): return (lax.ppermute(last, axis, up), lax.ppermute(initial, axis, down))  7.56 us
    unnamed x16, local copies, waits for them, and re-layouts  6.23 us
    pallas_call x1, Pallas kernels, make_table(): pl.pallas_call(functools.partial(table_kernel, nx, ny, tiles_east, tiles_...  5.61 us
    pallas_call x1, Pallas kernels, apply_mix(): pl.pallas_call(apply_kernel, out_shape=jax.ShapeDtypeStruct((rows, feat),...  3.99 us
  transfers between devices with their start and end apart: 4, of which 0 were waited for; matrix products, arithmetic and copies ran while one was open for 6% of the time, Pallas kernels for 15%

profile of v3, /device:TPU:0, one launch (start us, length us, event | category | flops | bytes accessed | tf_op | source)
XLA Modules:
  0.0 99.5 jit_solution(9800769625338299097)
XLA Ops:
  0.0 1.0 %fusion.1 = (f32[2,64,384]{2,1,0:T(8,128)S(1)}, f32[2,64,384]{2,1,0:T(8,128)S(1)}) fusion(f32[32,64,384]{2,1,0:T(8,128)} %state_ref.1), kind=kLoop, calls=%fused_computation.3 | loop fusion | bytes 786432 | tf_op jit(solution)/shard_map/slice | solution.py:481
  1.1 5.5 %collective-permute-start.1 = (f32[2,64,384]{2,1,0:T(8,128)S(1)}, f32[2,64,384]{2,1,0:T(8,128)S(1)}, u32[]{:S(2)}, u32[]{:S(2)}) collective-permute-start(f32[2,64,384]{2,1,0:T(8,128)S(1)} %get-tuple-element.17), channel_id=1, source_target_pairs={{2,0},{4,2},{6,4},{8,6},{10,8},{12,10},{14,12},{16,14},{18,16},{20... | collective-permute-start | bytes 589832 | tf_op jit(solution)/shard_map/ppermute | solution.py:406
  6.5 0.7 convert_element_type.16
  7.3 1.4 %reshape.28.owner_ref = s32[64,128]{1,0:T(8,128)} reshape(s32[2,4096]{1,0:T(2,128)} %owner_ref.1) | data formatting | bytes 65536 | tf_op jit(solution)/shard_map/reshape | solution.py:114
  8.7 0.6 pad.4.pattern_ref
  9.3 9.4 %shard_map.82 = (f32[32,1,128]{2,1,0:T(1,128)}, s32[64,128]{1,0:T(8,128)}) custom-call(f32[1,128]{1,0:T(1,128)} %pad.4.pattern_ref, s32[64,128]{1,0:T(8,128)} %reshape.28.owner_ref), custom_call_target="tpu_custom_call" | custom-call | tf_op jit(solution)/shard_map/pallas_call | solution.py:115
  18.7 1.2 %fusion = (f32[32,2,384]{2,1,0:T(2,128)S(1)}, f32[32,2,384]{2,1,0:T(2,128)S(1)}) fusion(f32[32,64,384]{2,1,0:T(8,128)} %state_ref.1), kind=kLoop, calls=%fused_computation.2 | loop fusion | bytes 393216 | tf_op jit(solution)/shard_map/slice | solution.py:484
  20.1 1.4 %collective-permute-start.2 = (f32[36,2,384]{2,1,0:T(2,128)S(1)}, f32[36,2,384]{2,1,0:T(2,128)S(1)}, u32[]{:S(2)}, u32[]{:S(2)}) collective-permute-start(f32[36,2,384]{2,1,0:T(2,128)S(1)} %get-tuple-element.11), channel_id=1, source_target_pairs={{0,1},{1,0},{2,3},{3,2},{4,5},{5,4},{6,7},{7,6},{8,9},{9,8},{10,11... | collective-permute-start | bytes 331784 | tf_op jit(solution)/shard_map/ppermute | solution.py:406
  21.5 0.7 collective-permute-start.3
  22.1 0.8 copy.11
  22.9 1.0 copy.10
  23.9 0.7 copy-done.1
  24.7 0.8 copy-done.2
  25.4 0.8 copy-done.3
  26.2 0.8 copy-done.4
  27.0 0.8 copy-done.5
  27.7 0.7 copy-done.6
  28.4 5.6 %shard_map.84.table_ref = f32[4096,128]{1,0:T(8,128)S(1)} custom-call(s32[2,4096]{1,0:T(2,128)S(1)} %copy-done.1, s32[2,4096]{1,0:T(2,128)S(1)} %copy-done.2, s32[2,4096]{1,0:T(2,128)S(1)} %copy-done.3, f32[6,4096]{1,0:T(8,128)S(1)} %reshape.30.coef_ref, f32[2,4096]{1,0:T(2,128)S(1)} %copy-done.4, f32[2,4096]{1,0:T(2,128)S(1)} %copy-done.5, ...), custom_call_target="tpu_custom_call" | custom-call | flops 50000000 | bytes 12000000 | tf_op jit(solution)/shard_map/pallas_call | solution.py:464
  34.1 8.7 %shard_map.83.field_ref = f32[2048,384]{1,0:T(8,128)S(1)} custom-call(f32[32,64,384]{2,1,0:T(8,128)} %state_ref.1, f32[2,64,384]{2,1,0:T(8,128)S(1)} %collective-permute-done.west_ref, f32[2,64,384]{2,1,0:T(8,128)S(1)} %collective-permute-done.1.east_ref, f32[36,2,384]{2,1,0:T(2,128)S(1)} %collective-permute-done.2.south_ref, ...), custom_call_target="tpu_custom_call" | custom-call | tf_op jit(solution)/shard_map/pallas_call | solution.py:177
  42.8 5.9 %shard_map.85.x_ref = f32[32,9,128]{2,1,0:T(8,128)S(1)} custom-call(s32[64,128]{1,0:T(8,128)S(1)} %copy-done, s32[8192]{0:T(1024)S(1)} %bitcast.4, f32[2048,384]{1,0:T(8,128)S(1)} %shard_map.83.field_ref, f32[4096,128]{1,0:T(8,128)S(1)} %shard_map.84.table_ref), custom_call_target="tpu_custom_call" | custom-call | tf_op jit(solution)/shard_map/pallas_call | solution.py:281
  48.7 18.2 %shard_map.86.rest_0_.one_ref = f32[128,128]{1,0:T(8,128)S(1)} custom-call(f32[32,9,128]{2,1,0:T(8,128)S(1)} %shard_map.85.x_ref), custom_call_target="tpu_custom_call" | custom-call | tf_op jit(solution)/shard_map/pallas_call | solution.py:361
  66.9 6.4 %shard_map.87.x_ref = f32[32,9,128]{2,1,0:T(8,128)S(1)} custom-call(s32[64,128]{1,0:T(8,128)S(1)} %copy-done, s32[8192]{0:T(1024)S(1)} %bitcast.5, f32[2048,384]{1,0:T(8,128)S(1)} %shard_map.83.field_ref, f32[4096,128]{1,0:T(8,128)S(1)} %shard_map.84.table_ref, f32[128,128]{1,0:T(8,128)S(1)} %shard_map.86.rest_0_.one_ref), custom_call_target="tpu_custom_call" | custom-call | tf_op jit(solution)/shard_map/pallas_call | solution.py:281
  73.4 22.1 %shard_map.88.two_ref = f32[128,128]{1,0:T(8,128)S(1)} custom-call(f32[32,9,128]{2,1,0:T(8,128)S(1)} %shard_map.87.x_ref), custom_call_target="tpu_custom_call" | custom-call | tf_op jit(solution)/shard_map/pallas_call | solution.py:361
  95.5 4.0 %shard_map.89 = f32[2048,384]{1,0:T(8,128)} custom-call(f32[2048,384]{1,0:T(8,128)S(1)} %shard_map.83.field_ref, f32[128,128]{1,0:T(8,128)S(1)} %shard_map.86.rest_0_.one_ref, f32[128,128]{1,0:T(8,128)S(1)} %shard_map.88.two_ref), custom_call_target="tpu_custom_call" | custom-call | tf_op jit(solution)/shard_map/pallas_call | solution.py:388
  (18 shorter events, 0.3 us)
Async XLA Ops:
  1.1 18.8 %collective-permute-start.1 = (f32[2,64,384]{2,1,0:T(8,128)S(1)}, f32[2,64,384]{2,1,0:T(8,128)S(1)}, u32[]{:S(2)}, u32[]{:S(2)}) collective-permute-start(f32[2,64,384]{2,1,0:T(8,128)S(1)} %get-tuple-element.17), channel_id=1, source_target_pairs={{2,0},{4,2},{6,4},{8,6},{10,8},{12,10},{14,12},{16,14},{18,16},{20... | collective-permute-start | bytes 589832 | tf_op jit(solution)/shard_map/ppermute | solution.py:406
  6.5 13.4 %collective-permute-start = (f32[2,64,384]{2,1,0:T(8,128)S(1)}, f32[2,64,384]{2,1,0:T(8,128)S(1)}, u32[]{:S(2)}, u32[]{:S(2)}) collective-permute-start(f32[2,64,384]{2,1,0:T(8,128)S(1)} %get-tuple-element.18), channel_id=1, source_target_pairs={{0,2},{2,4},{4,6},{6,8},{8,10},{10,12},{12,14},{14,16},{16,18},{18... | collective-permute-start | bytes 589832 | tf_op jit(solution)/shard_map/ppermute | solution.py:406
  20.1 14.0 %collective-permute-start.2 = (f32[36,2,384]{2,1,0:T(2,128)S(1)}, f32[36,2,384]{2,1,0:T(2,128)S(1)}, u32[]{:S(2)}, u32[]{:S(2)}) collective-permute-start(f32[36,2,384]{2,1,0:T(2,128)S(1)} %get-tuple-element.11), channel_id=1, source_target_pairs={{0,1},{1,0},{2,3},{3,2},{4,5},{5,4},{6,7},{7,6},{8,9},{9,8},{10,11... | collective-permute-start | bytes 331784 | tf_op jit(solution)/shard_map/ppermute | solution.py:406
  21.5 12.6 %collective-permute-start.3 = (f32[36,2,384]{2,1,0:T(2,128)S(1)}, f32[36,2,384]{2,1,0:T(2,128)S(1)}, u32[]{:S(2)}, u32[]{:S(2)}) collective-permute-start(f32[36,2,384]{2,1,0:T(2,128)S(1)} %get-tuple-element.12), channel_id=1, source_target_pairs={{1,0},{0,1},{3,2},{2,3},{5,4},{4,5},{7,6},{6,7},{9,8},{8,9},{11,10... | collective-permute-start | bytes 331784 | tf_op jit(solution)/shard_map/ppermute | solution.py:406
  23.9 0.8 copy-start.1
  24.7 0.8 copy-start.2
  25.4 0.8 copy-start.3
  26.2 0.8 copy-start.4
  27.0 0.8 copy-start.5
  27.7 0.7 copy-start.6
  34.1 8.8 %copy-start = (s32[64,128]{1,0:T(8,128)S(1)}, s32[64,128]{1,0:T(8,128)}, u32[]{:S(2)}) copy-start(s32[64,128]{1,0:T(8,128)} %get-tuple-element.13.list_ref) | copy-start | bytes 98308
